TPU v7x, 256 devices: a whole 4x4x8 slice. The times are simulated.
256 devices in a mesh: fsdp: 16 (over x_lo, z), seq: 16 (over y, x_hi, core).
Axes of the slice: x: 4 (x_hi: 2, x_lo: 2; x = x_hi * 2 + x_lo), y: 4, z: 8, core: 2. Of those that a mesh axis runs over, the one named last changes fastest.
Arguments:
- normed_input: bfloat16 [16, 2048, 2048], P('fsdp', 'seq'), may hold values from -40 to 40
- out_grad: bfloat16 [16, 2048, 2048], P('fsdp', 'seq'), may hold values from -6 to 6
- w_query: bfloat16 [2048, 2048], P('fsdp', 'seq'), may hold values from -1 to 1
- key_weight_matrix: bfloat16 [2048, 512], P('fsdp'), may hold values from -1 to 1
- value_weight_matrix: bfloat16 [2048, 512], P('fsdp'), may hold values from -0.125 to 0.125
- boundary: int32 [16], P('fsdp'), may hold values from 1 to 2047
Outputs:
- input_grad: bfloat16 [16, 2048, 2048], P('fsdp', 'seq')
- grad_query_w: float32 [2048, 2048], P('fsdp', 'seq')
- grad_key_w: float32 [2048, 512], P('fsdp')
- grad_value_w: float32 [2048, 512], P('fsdp')
All inputs are finite; a program needn't handle non-finite values.
Results may differ from a plain program's by a relative error of at most 0.034.
The roundings to bfloat16 on the way count: a program that leaves them out, or rounds other values in their place, can miss the bound.
Values may be sent and summed in bfloat16 or wider, within the bound.
A program may use at most 64 MiB of HBM per device.

v0:
```python
import jax
import jax.numpy as jnp
from jax import lax
from jax.sharding import PartitionSpec as P

QUERY_HEADS = 16
KEY_VALUE_HEADS = 4
HEAD_SIZE = 128


def rope_tables(length):
    half_size = HEAD_SIZE // 2
    inverse = 500000.0 ** (-(jnp.arange(half_size, dtype=jnp.float32) * 2.0 / HEAD_SIZE))
    angles = jnp.arange(length, dtype=jnp.float32)[:, None] * inverse[None, :]
    return (jnp.cos(angles), jnp.sin(angles))


def apply_rotation(values, cosine_lookup, sine_lookup):
    half_size = values.shape[-1] // 2
    first_half = values[..., :half_size]
    second_half = values[..., half_size:]
    cosine_part = cosine_lookup[:, None, :]
    sine_part = sine_lookup[:, None, :]
    return jnp.concatenate(
        [
            first_half * cosine_part - second_half * sine_part,
            second_half * cosine_part + first_half * sine_part,
        ],
        axis=-1,
    )


def shards(normed_input, out_grad, w_query, key_weight_matrix, value_weight_matrix, boundary):
    seq_count = lax.axis_size("seq")
    seq_index = lax.axis_index("seq")
    tok_rows = normed_input.shape[1]
    length = tok_rows * seq_count
    feature_width = normed_input.shape[2]
    head_count = w_query.shape[1] // HEAD_SIZE
    group_count = QUERY_HEADS // KEY_VALUE_HEADS
    kv_heads = max(1, head_count // group_count)
    per_kv = head_count // kv_heads
    query_feature_width = head_count * HEAD_SIZE
    key_width = kv_heads * HEAD_SIZE
    leading_key_value = seq_index * head_count // group_count
    key_cols = lax.dynamic_slice_in_dim(
        key_weight_matrix, leading_key_value * HEAD_SIZE, key_width, 1
    )
    value_cols = lax.dynamic_slice_in_dim(
        value_weight_matrix, leading_key_value * HEAD_SIZE, key_width, 1
    )
    query_full, key_full, value_full = (
        lax.all_gather(w_query, "fsdp", axis=0, tiled=True),
        lax.all_gather(key_cols, "fsdp", axis=0, tiled=True),
        lax.all_gather(value_cols, "fsdp", axis=0, tiled=True),
    )
    own_weights = jnp.concatenate([query_full, key_full, value_full], axis=1)
    local_rows = normed_input[0]
    grad_split = out_grad[0].reshape(tok_rows, seq_count, query_feature_width)
    grad_heads = lax.all_to_all(grad_split, "seq", split_axis=1, concat_axis=0, tiled=True)
    all_rows = lax.all_gather(local_rows, "seq", axis=0, tiled=True)
    projected = jnp.dot(all_rows, own_weights, preferred_element_type=jnp.float32)
    cosine_lookup, sine_lookup = rope_tables(length)
    queries = apply_rotation(
        projected[:, :query_feature_width].reshape(length, head_count, HEAD_SIZE),
        cosine_lookup,
        sine_lookup,
    ).astype(jnp.bfloat16)
    key_head_rows = apply_rotation(
        projected[:, query_feature_width : query_feature_width + key_width].reshape(
            length, kv_heads, HEAD_SIZE
        ),
        cosine_lookup,
        sine_lookup,
    ).astype(jnp.bfloat16)
    value_head_rows = (
        projected[:, query_feature_width + key_width :]
        .astype(jnp.bfloat16)
        .reshape(length, kv_heads, HEAD_SIZE)
    )
    key_head_rows = jnp.repeat(key_head_rows, per_kv, axis=1)
    value_head_rows = jnp.repeat(value_head_rows, per_kv, axis=1)
    book_start = boundary[0]
    block_rows = min(512, length)
    score_scale = HEAD_SIZE ** (-0.5)
    positions = jnp.arange(length, dtype=jnp.int32)
    query_grads = []
    key_grads = jnp.zeros((length, head_count, HEAD_SIZE), jnp.float32)
    value_grads = jnp.zeros((length, head_count, HEAD_SIZE), jnp.float32)
    for block_index in range((length + block_rows - 1) // block_rows):
        block_start = block_index * block_rows
        block_end = min(block_start + block_rows, length)
        query_block = queries[block_start:block_end]
        key_prefix = key_head_rows[:block_end]
        value_prefix = value_head_rows[:block_end]
        grad_block = grad_heads[block_start:block_end]
        query_pos = positions[block_start:block_end][:, None]
        key_pos = positions[:block_end][None, :]
        allowed = (key_pos <= query_pos) & ((query_pos < book_start) == (key_pos < book_start))
        scores = (
            jnp.einsum("qhd,khd->hqk", query_block, key_prefix, preferred_element_type=jnp.float32)
            * score_scale
        )
        scores = jnp.where(allowed[None], scores, -1e30)
        row_max = jnp.max(scores, axis=-1, keepdims=True)
        exponent = jnp.exp(scores - row_max)
        prob_full = exponent / jnp.sum(exponent, axis=-1, keepdims=True)
        prob_low = prob_full.astype(jnp.bfloat16)
        context = jnp.einsum(
            "hqk,khd->qhd", prob_low, value_prefix, preferred_element_type=jnp.float32
        )
        row_delta = jnp.sum(grad_block.astype(jnp.float32) * context, axis=-1)
        prob_grad = jnp.einsum(
            "qhd,khd->hqk", grad_block, value_prefix, preferred_element_type=jnp.float32
        )
        score_grad = (prob_full * (prob_grad - row_delta.T[:, :, None])).astype(jnp.bfloat16)
        query_grads.append(
            jnp.einsum("hqk,khd->qhd", score_grad, key_prefix, preferred_element_type=jnp.float32)
            * score_scale
        )
        key_grads = key_grads.at[:block_end].add(
            jnp.einsum("hqk,qhd->khd", score_grad, query_block, preferred_element_type=jnp.float32)
            * score_scale
        )
        value_grads = value_grads.at[:block_end].add(
            jnp.einsum("hqk,qhd->khd", prob_low, grad_block, preferred_element_type=jnp.float32)
        )
    query_grad = apply_rotation(
        jnp.concatenate(query_grads, axis=0), cosine_lookup, -sine_lookup
    ).astype(jnp.bfloat16)
    key_grad = apply_rotation(key_grads, cosine_lookup, -sine_lookup).astype(jnp.bfloat16)
    value_grad = value_grads.astype(jnp.bfloat16)
    grad_cols = jnp.concatenate(
        [
            query_grad.reshape(length, query_feature_width),
            key_grad.reshape(length, query_feature_width),
            value_grad.reshape(length, query_feature_width),
        ],
        axis=1,
    )
    contract = (((0,), (0,)), ((), ()))
    weight_gradient = lax.dot_general(
        all_rows, grad_cols, contract, preferred_element_type=jnp.float32
    )
    own_query_grad = weight_gradient[:, :query_feature_width]
    local_key_gradient = (
        weight_gradient[:, query_feature_width : 2 * query_feature_width]
        .reshape(feature_width, kv_heads, per_kv, HEAD_SIZE)
        .sum(axis=2)
        .reshape(feature_width, key_width)
    )
    local_value_gradient = (
        weight_gradient[:, 2 * query_feature_width :]
        .reshape(feature_width, kv_heads, per_kv, HEAD_SIZE)
        .sum(axis=2)
        .reshape(feature_width, key_width)
    )
    grad_query_w = lax.psum_scatter(
        own_query_grad.astype(jnp.bfloat16), "fsdp", scatter_dimension=0, tiled=True
    ).astype(jnp.float32)
    padded_key = lax.dynamic_update_slice_in_dim(
        jnp.zeros((feature_width, KEY_VALUE_HEADS * HEAD_SIZE), jnp.float32),
        local_key_gradient,
        leading_key_value * HEAD_SIZE,
        1,
    )
    padded_value = lax.dynamic_update_slice_in_dim(
        jnp.zeros((feature_width, KEY_VALUE_HEADS * HEAD_SIZE), jnp.float32),
        local_value_gradient,
        leading_key_value * HEAD_SIZE,
        1,
    )
    key_part, value_part = (
        lax.psum_scatter(
            padded_key.astype(jnp.bfloat16), "fsdp", scatter_dimension=0, tiled=True
        ).astype(jnp.float32),
        lax.psum_scatter(
            padded_value.astype(jnp.bfloat16), "fsdp", scatter_dimension=0, tiled=True
        ).astype(jnp.float32),
    )
    grad_key_w, grad_value_w = (
        lax.psum(key_part.astype(jnp.bfloat16), "seq").astype(jnp.float32),
        lax.psum(value_part.astype(jnp.bfloat16), "seq").astype(jnp.float32),
    )
    key_expanded = jnp.repeat(
        key_full.reshape(feature_width, kv_heads, HEAD_SIZE), per_kv, axis=1
    ).reshape(feature_width, query_feature_width)
    value_expanded = jnp.repeat(
        value_full.reshape(feature_width, kv_heads, HEAD_SIZE), per_kv, axis=1
    ).reshape(feature_width, query_feature_width)
    wide_weights = jnp.concatenate([query_full, key_expanded, value_expanded], axis=1)
    input_grad = lax.psum_scatter(
        lax.dot_general(
            grad_cols, wide_weights, (((1,), (1,)), ((), ())), preferred_element_type=jnp.float32
        ).astype(jnp.bfloat16),
        "seq",
        scatter_dimension=0,
        tiled=True,
    )
    return (input_grad[None], grad_query_w, grad_key_w, grad_value_w)


def solution(mesh):
    return jax.shard_map(
        shards,
        mesh=mesh,
        in_specs=(
            P("fsdp", "seq", None),
            P("fsdp", "seq", None),
            P("fsdp", "seq"),
            P("fsdp", None),
            P("fsdp", None),
            P("fsdp"),
        ),
        out_specs=(P("fsdp", "seq", None), P("fsdp", "seq"), P("fsdp", None), P("fsdp", None)),
        check_vma=False,
    )
```

profile of v0, /device:TPU:1, one launch (start us, length us, event | category | flops | bytes accessed | tf_op | source)
XLA Modules:
  0.0 646.6 jit_solution(16322845858614552770)
XLA Ops:
  7.9 2.0 copy.28
  10.0 8.4 %all-to-all-start = ((bf16[128,16,128]{0,2,1:T(8,128)(2,1)}), bf16[128,16,128]{0,2,1:T(8,128)(2,1)S(1)}, u32[]{:S(2)}, u32[]{:S(2)}) async-start(bf16[128,16,128]{0,2,1:T(8,128)(2,1)} %bitcast.7), calls=%async_computation | async-start | bytes 1048576 | tf_op jit(solution)/shard_map/all_to_all | solution.py:60
  19.3 0.8 constant_dynamic-slice_fusion
  20.1 32.4 %all_gather.12 = bf16[2048,128]{1,0:T(8,128)(2,1)S(1)} all-gather(bf16[128,128]{1,0:T(8,128)(2,1)S(1)} %copy-done.6), channel_id=1, replica_groups=mesh['fsdp'=16,'seq'=16] {'fsdp'}, dimensions={0}, use_global_device_ids=true | all-gather | bytes 557056 | tf_op jit(solution)/shard_map/all_gather | solution.py:53
  52.6 27.8 %all_gather.13 = bf16[2048,128]{1,0:T(8,128)(2,1)S(1)} all-gather(bf16[128,128]{1,0:T(8,128)(2,1)S(1)} %constant_dynamic-slice_fusion.1), channel_id=1, replica_groups=mesh['fsdp'=16,'seq'=16] {'fsdp'}, dimensions={0}, use_global_device_ids=true | all-gather | bytes 557056 | tf_op jit(solution)/shard_map/all_gather | solution.py:54
  80.5 27.3 %all_gather.14 = bf16[2048,128]{1,0:T(8,128)(2,1)S(1)} all-gather(bf16[128,128]{1,0:T(8,128)(2,1)S(1)} %constant_dynamic-slice_fusion), channel_id=1, replica_groups=mesh['fsdp'=16,'seq'=16] {'fsdp'}, dimensions={0}, use_global_device_ids=true | all-gather | bytes 557056 | tf_op jit(solution)/shard_map/all_gather | solution.py:55
  109.2 5.9 fusion.105
  115.3 2.6 subtract_convert_fusion.3
  120.2 1.0 fusion.106
  129.7 1.4 fusion.104
  131.8 0.8 fusion.6
  132.7 1.1 fusion.55
  134.5 0.8 fusion.44
  135.9 2.3 bitcast_dynamic-update-slice_fusion.3
  138.2 2.3 bitcast_dynamic-update-slice_fusion.2
  140.6 2.3 bitcast_dynamic-update-slice_fusion.1
  142.9 2.3 bitcast_dynamic-update-slice_fusion
  145.7 3.4 fusion.15
  149.2 0.9 fusion.102
  150.7 1.3 copy-done.3
  152.1 1.3 copy.37
  153.7 1.3 copy-done.2
  155.1 1.0 copy.47
  156.1 74.5 %reduce-scatter.11.cloned.1.call-done = bf16[128,512]{1,0:T(8,128)(2,1)} async-done(((bf16[2048,512]{1,0:T(8,128)(2,1)}), bf16[128,512]{1,0:T(8,128)(2,1)}) %reduce-scatter.11.cloned.1.call-update) | async-done | bytes 131088 | tf_op jit(solution)/shard_map/reduce_scatter | solution.py:177
  230.6 73.1 %reduce-scatter.9.cloned.1.call-done = bf16[128,512]{1,0:T(8,128)(2,1)} async-done(((bf16[2048,512]{1,0:T(8,128)(2,1)}), bf16[128,512]{1,0:T(8,128)(2,1)}) %reduce-scatter.9.cloned.1.call-update) | async-done | bytes 131088 | tf_op jit(solution)/shard_map/reduce_scatter | solution.py:174
  304.0 9.7 %convolution_convert_fusion = bf16[2048,2048]{1,0:T(8,128)(2,1)} fusion(bf16[2048,384]{0,1:T(8,128)(2,1)} %copy-done.5, bf16[2048,384]{1,0:T(8,128)(2,1)} %copy-done.4), kind=kOutput, calls=%fused_computation.4 | convolution fusion | flops 3225419776 | bytes 11534336 | tf_op jit(solution)/shard_map/dot_general | solution.py:193
  313.8 58.2 %reduce-scatter.13.cloned.1.call-done = bf16[128,128]{1,0:T(8,128)(2,1)} async-done(((bf16[2048,128]{1,0:T(8,128)(2,1)}), bf16[128,128]{1,0:T(8,128)(2,1)}) %reduce-scatter.13.cloned.1.call-update) | async-done | bytes 32784
  371.9 0.9 copy.48
  373.6 151.0 %all-reduce.5.cloned.1.call-done = (bf16[128,512]{1,0:T(8,128)(2,1)}, bf16[128,512]{1,0:T(8,128)(2,1)}) async-done(((bf16[128,512]{1,0:T(8,128)(2,1)}, bf16[128,512]{1,0:T(8,128)(2,1)}), (bf16[128,512]{1,0:T(8,128)(2,1)}, bf16[128,512]{1,0:T(8,128)(2,1)})) %all-reduce.5.cloned.1.call-update) | async-done | bytes 262160 | tf_op jit(solution)/shard_map/psum | solution.py:182
  524.6 1.6 convert_element_type.163
  526.2 1.6 convert_element_type.165
  527.8 111.9 %reduce-scatter.7.cloned.1.call-done = bf16[128,2048]{1,0:T(8,128)(2,1)} async-done(((bf16[2048,2048]{1,0:T(8,128)(2,1)}), bf16[128,2048]{1,0:T(8,128)(2,1)}) %reduce-scatter.7.cloned.1.call-update) | async-done | bytes 524304 | tf_op jit(solution)/shard_map/reduce_scatter | solution.py:192
  (92 shorter events, 17.7 us)
Async XLA Ops:
  7.2 12.1 %copy-start = (bf16[128,512]{1,0:T(8,128)(2,1)S(1)}, bf16[128,512]{1,0:T(8,128)(2,1)}, u32[]{:S(2)}) copy-start(bf16[128,512]{1,0:T(8,128)(2,1)} %param.29) | copy-start | bytes 393220
  7.2 12.9 %copy-start.6 = (bf16[128,128]{1,0:T(8,128)(2,1)S(1)}, bf16[128,128]{1,0:T(8,128)(2,1)}, u32[]{:S(2)}) copy-start(bf16[128,128]{1,0:T(8,128)(2,1)} %param.28) | copy-start | bytes 98308
  7.2 101.8 %all-gather.3.cloned.1.call-start = ((), (), s32[]{:S(2)}) async-start(), calls=%async_computation.8 | async-start | bytes 8912896 | tf_op jit(solution)/shard_map/all_gather | solution.py:61
  10.0 98.0 %all-to-all-start = ((bf16[128,16,128]{0,2,1:T(8,128)(2,1)}), bf16[128,16,128]{0,2,1:T(8,128)(2,1)S(1)}, u32[]{:S(2)}, u32[]{:S(2)}) async-start(bf16[128,16,128]{0,2,1:T(8,128)(2,1)} %bitcast.7), calls=%async_computation | async-start | bytes 1048576 | tf_op jit(solution)/shard_map/all_to_all | solution.py:60
  18.4 212.2 %reduce-scatter.11.cloned.1.call-start = ((), (), s32[]{:S(2)}) async-start(), calls=%async_computation.7 | async-start | bytes 2228224 | tf_op jit(solution)/shard_map/reduce_scatter | solution.py:177
  108.0 1.2 copy-start.4
  135.3 10.4 %slice-start = ((s8[8388608]{0:T(1024)(128)(4,1)}), s8[4194304]{0:T(1024)(128)(4,1)S(1)}, s32[]{:S(2)}) async-start(s8[8388608]{0:T(1024)(128)(4,1)} %bitcast.268), calls=%async_computation.11 | async-start | bytes 8388608
  138.2 7.5 %slice-start.1 = ((s8[8388608]{0:T(1024)(128)(4,1)}), s8[4194304]{0:T(1024)(128)(4,1)S(1)}, s32[]{:S(2)}) async-start(s8[8388608]{0:T(1024)(128)(4,1)} %bitcast.268), calls=%async_computation.12 | async-start | bytes 8388608
  145.7 3.4 copy-start.5
  150.7 1.4 copy-start.3
  152.0 151.7 %reduce-scatter.9.cloned.1.call-start = ((), (), s32[]{:S(2)}) async-start(), calls=%async_computation.6 | async-start | bytes 2228224 | tf_op jit(solution)/shard_map/reduce_scatter | solution.py:174
  153.7 1.3 copy-start.2
  155.0 216.9 %reduce-scatter.13.cloned.1.call-start = ((), (), s32[]{:S(2)}) async-start(), calls=%async_computation.9 | async-start | bytes 557056
  156.1 368.5 %all-reduce.5.cloned.1.call-start = ((), (), s32[]{:S(2)}) async-start(), calls=%async_computation.10 | async-start | bytes 524288 | tf_op jit(solution)/shard_map/psum | solution.py:182
  303.7 336.0 %reduce-scatter.7.cloned.1.call-start = ((), (), s32[]{:S(2)}) async-start(), calls=%async_computation.5 | async-start | bytes 8912896 | tf_op jit(solution)/shard_map/reduce_scatter | solution.py:192
  313.7 326.0 %copy-start.1 = (bf16[128,512]{1,0:T(8,128)(2,1)S(1)}, bf16[128,512]{1,0:T(8,128)(2,1)}, u32[]{:S(2)}) copy-start(bf16[128,512]{1,0:T(8,128)(2,1)} %param.29) | copy-start | bytes 393220
Sparse Core Ops, SparseCore 0:
  10.8 87.4 all-gather.2
  152.2 78.4 reduce-scatter.10
  233.2 70.4 reduce-scatter.8
  306.0 65.8 reduce-scatter.12
  374.6 149.8 all-reduce.4
  529.6 110.1 reduce-scatter.6
where the time goes:
time: 647 us
  waiting for transfers between devices  469 us (72%)
  blocking collectives  87.5 us (14%)
  matrix products  33.3 us (5%)
  other arithmetic  19.1 us (3%)
  between operations  15.4 us (2%)
  local copies, waits for them, and re-layouts  12.9 us (2%)
  starting transfers between devices  8.95 us (1%)
    psum x1, waiting for transfers between devices, shards(): lax.psum(key_part.astype(jnp.bfloat16), 'seq').astype(jnp.float32)  151 us
    reduce_scatter x1, waiting for transfers between devices, shards(): lax.psum_scatter(lax.dot_general(grad_cols, wide_weights, (((1,), (1,)),...  112 us
    reduce_scatter x1, waiting for transfers between devices, shards(): lax.psum_scatter(padded_value.astype(jnp.bfloat16), 'fsdp', scatter_dimen...  74.5 us
    reduce_scatter x1, waiting for transfers between devices, shards(): lax.psum_scatter(padded_key.astype(jnp.bfloat16), 'fsdp', scatter_dimensi...  73.1 us
    unnamed x7, waiting for transfers between devices  59 us
    all_gather x1, blocking collectives, shards(): lax.all_gather(w_query, 'fsdp', axis=0, tiled=True)  32.4 us
    all_gather x1, blocking collectives, shards(): lax.all_gather(key_cols, 'fsdp', axis=0, tiled=True)  27.8 us
    all_gather x1, blocking collectives, shards(): lax.all_gather(value_cols, 'fsdp', axis=0, tiled=True)  27.3 us
  transfers between devices with their start and end apart: 7, of which 5 were waited for; matrix products, arithmetic and copies ran while one was open for 3% of the time, Pallas kernels for 0%

commit v1 on v0

v1 whole, which is shorter than its diff:
```python
import functools

import jax
import jax.numpy as jnp
import numpy as np
from jax import lax
from jax.experimental import pallas as pl
from jax.experimental.pallas import tpu as pltpu
from jax.sharding import PartitionSpec as P

HEAD = 128
N_SEQ = 16
N_FSDP = 16
ROWS = 128
LENGTH = 2048
FEATURES = 2048
GROUP = 4
MESH = pl.DeviceIdType.MESH
SCALE = HEAD ** (-0.5)
EXP2_SCALE = SCALE * 1.4426950408889634

GATHER = (
    ("up", (0, 0), 0, 64, (-1, 0)),
    ("down", (0, 0), 64, 64, (1, 0)),
    ("side", (0, 0), 0, 64, (0, 1)),
    ("up", (0, 0), 64, 64, (-1, 0)),
    ("down", (0, 0), 0, 64, (1, 0)),
    ("side", (0, 0), 64, 64, (0, 1)),
    ("up", (-1, 0), 0, 64, (2, 0)),
    ("down", (1, 0), 64, 64, (2, 0)),
    ("side", (-1, 0), 0, 64, (-1, 1)),
    ("side", (1, 0), 64, 64, (1, 1)),
    ("down", (0, 1), 0, 64, (1, 1)),
    ("up", (0, 1), 64, 64, (-1, 1)),
    ("up", (-1, 1), 0, 48, (2, 1)),
    ("down", (1, 1), 80, 48, (2, 1)),
    ("side", (2, 0), 48, 32, (2, 1)),
)

REDUCE = (
    ("down", (2, 1), 0, 48, (-1, 1)),
    ("up", (2, 1), 80, 48, (1, 1)),
    ("side", (2, 1), 48, 32, (2, 0)),
    ("side", (-1, 1), 0, 64, (-1, 0)),
    ("side", (1, 1), 64, 64, (1, 0)),
    ("down", (-1, 1), 64, 64, (0, 1)),
    ("up", (1, 1), 0, 64, (0, 1)),
    ("down", (2, 0), 0, 64, (-1, 0)),
    ("up", (2, 0), 64, 64, (1, 0)),
    ("side", (0, 1), 0, 128, (0, 0)),
    ("down", (-1, 0), 0, 128, (0, 0)),
    ("up", (1, 0), 0, 128, (0, 0)),
)


class Place:
    def __init__(self):
        self.f = lax.axis_index("fsdp")
        self.s = lax.axis_index("seq")
        self.core = lax.rem(self.s, 2)
        self.hi = lax.rem(lax.div(self.s, 2), 2)
        self.y = lax.div(self.s, 4)
        self.z = lax.rem(self.f, 8)
        self.lo = lax.div(self.f, 8)

    def to(self, direction):
        s = self.s
        if direction == "up":
            return (self.f, lax.rem(s + 4, N_SEQ))
        if direction == "down":
            return (self.f, lax.rem(s + 12, N_SEQ))
        if direction == "side":
            return (self.f, s + 2 - 4 * self.hi)
        return (self.f, s + 1 - 2 * self.core)

    def block(self, rel, other_core=0):
        dy, dh = rel
        y = lax.rem(self.y + dy + 4, 4)
        hi = 1 - self.hi if dh else self.hi
        core = 1 - self.core if other_core else self.core
        return y * 4 + hi * 2 + core


def enter(place, fsdp_peers):
    barrier = pltpu.get_barrier_semaphore()

    def greet(j, carry):
        pl.semaphore_signal(
            barrier,
            inc=1,
            device_id=(place.f, lax.rem(place.s + j, N_SEQ)),
            device_id_type=MESH,
        )
        pl.semaphore_signal(
            barrier,
            inc=1,
            device_id=(lax.rem(place.f + j, N_FSDP), place.s),
            device_id_type=MESH,
        )
        return carry

    lax.fori_loop(1, N_SEQ, greet, 0)
    pl.semaphore_wait(barrier, 2 * (N_SEQ - 1))


def remote(src, dst, send, recv, device):
    return pltpu.make_async_remote_copy(
        src_ref=src,
        dst_ref=dst,
        send_sem=send,
        recv_sem=recv,
        device_id=device,
        device_id_type=MESH,
    )


def gather_kernel(
    x_ref, g_ref, wq_ref, wk_ref, wv_ref, cos_ref, sin_ref,
    rows_out, q_ref, k_ref, v_ref, grad_ref, w_ref,
    rows, kv, x_send, x_recv, c_send, c_recv, g_send, g_recv, w_send, w_recv, o_sem,
):
    me = Place()
    own = pl.multiple_of(me.s * ROWS, ROWS)
    w_own = pl.multiple_of(me.f * ROWS, ROWS)
    kv_col = pl.multiple_of(HEAD + me.core * HEAD, HEAD)
    kv_other = pl.multiple_of(HEAD + (1 - me.core) * HEAD, HEAD)
    head_col = pl.multiple_of(me.y * HEAD, HEAD)
    kv[...] = jnp.where(
        me.core == 0,
        wk_ref[:, pl.ds(head_col, HEAD)].astype(jnp.float32),
        wv_ref[:, pl.ds(head_col, HEAD)].astype(jnp.float32),
    ).astype(jnp.bfloat16)
    w_ref[pl.ds(w_own, ROWS), :HEAD] = wq_ref[...]
    w_ref[pl.ds(w_own, ROWS), pl.ds(kv_col, HEAD)] = kv[...]
    rows[pl.ds(own, ROWS), :] = x_ref[...]
    grad_ref[pl.ds(own, ROWS), :] = g_ref[:, pl.ds(own, HEAD)]
    enter(me, True)

    def w_copies(j, device_f, source_f):
        at = pl.multiple_of(source_f * ROWS, ROWS)
        device = (device_f, me.s)
        return (
            remote(wq_ref, w_ref.at[pl.ds(at, ROWS), :HEAD], w_send.at[0, j], w_recv.at[0, j], device),
            remote(kv, w_ref.at[pl.ds(at, ROWS), pl.ds(kv_col, HEAD)], w_send.at[1, j], w_recv.at[1, j], device),
        )

    def w_start(j, carry):
        for copy in w_copies(j, lax.rem(me.f + j, N_FSDP), me.f):
            copy.start()
        return carry

    def part(rel, first, count, other_core=0):
        at = pl.multiple_of(me.block(rel, other_core) * ROWS + first, 16)
        return rows.at[pl.ds(at, count), :]

    def x_start(i):
        direction, rel, first, count, _ = GATHER[i]
        piece = part(rel, first, count)
        remote(piece, piece, x_send.at[i], x_recv.at[i], me.to(direction)).start()

    def x_arrived(i):
        direction, _, first, count, rel = GATHER[i]
        piece = part(rel, first, count)
        remote(piece, piece, x_send.at[i], x_recv.at[i], me.to(direction)).wait_recv()
        core_copy(i).start()

    def core_piece(i):
        if i == len(GATHER):
            return (0, 0), 0, 128
        _, _, first, count, rel = GATHER[i]
        return rel, first, count

    def core_copy(i, receive=False):
        piece = part(*core_piece(i), other_core=1 if receive else 0)
        return remote(piece, piece, c_send.at[i], c_recv.at[i], me.to("core"))

    def g_copy(j, device_s, source_s):
        at = pl.multiple_of(source_s * ROWS, ROWS)
        col = pl.multiple_of(device_s * HEAD, HEAD)
        return remote(
            g_ref.at[:, pl.ds(col, HEAD)],
            grad_ref.at[pl.ds(at, ROWS), :],
            g_send.at[j],
            g_recv.at[j],
            (me.f, device_s),
        )

    def g_start(j, carry):
        g_copy(j, lax.rem(me.s + j, N_SEQ), me.s).start()
        return carry

    for i in range(6):
        x_start(i)
    lax.fori_loop(1, N_FSDP, w_start, 0)
    core_copy(len(GATHER)).start()
    x_arrived(0)
    x_start(6)
    x_start(8)
    x_arrived(1)
    x_start(7)
    x_start(9)
    x_arrived(2)
    x_start(10)
    x_arrived(5)
    x_start(11)
    x_arrived(3)
    x_arrived(4)
    lax.fori_loop(1, N_SEQ, g_start, 0)
    x_arrived(8)
    x_start(12)
    x_arrived(9)
    x_start(13)
    x_arrived(6)
    x_arrived(7)
    x_start(14)

    def w_finish(j, carry):
        for copy in w_copies(j, lax.rem(me.f + N_FSDP - j, N_FSDP), lax.rem(me.f + N_FSDP - j, N_FSDP)):
            copy.wait_recv()
        for copy in w_copies(j, lax.rem(me.f + j, N_FSDP), me.f):
            copy.wait_send()
        return carry

    lax.fori_loop(1, N_FSDP, w_finish, 0)
    mine = w_ref.at[:, pl.ds(kv_col, HEAD)]
    theirs = w_ref.at[:, pl.ds(kv_other, HEAD)]
    share = remote(mine, mine, w_send.at[0, 0], w_recv.at[0, 0], me.to("core"))
    share.start()
    x_arrived(10)
    x_arrived(11)
    x_arrived(12)
    x_arrived(13)
    x_arrived(14)
    share.wait_send()
    remote(theirs, theirs, w_send.at[0, 0], w_recv.at[0, 0], me.to("core")).wait_recv()
    for i in range(len(GATHER) + 1):
        core_copy(i, True).wait_recv()
    save = pltpu.make_async_copy(rows, rows_out, o_sem.at[0])
    save.start()

    def project(c, carry):
        at = pl.ds(pl.multiple_of(c * 256, 256), 256)
        full = jnp.dot(rows[at, :], w_ref[...], preferred_element_type=jnp.float32)
        cos, sin = cos_ref[at, :], sin_ref[at, :]
        q, k = full[:, :HEAD], full[:, HEAD : 2 * HEAD]
        q_ref[at, :] = (q * cos + pltpu.roll(q, HEAD // 2, 1) * sin).astype(jnp.bfloat16)
        k_ref[at, :] = (k * cos + pltpu.roll(k, HEAD // 2, 1) * sin).astype(jnp.bfloat16)
        v_ref[at, :] = full[:, 2 * HEAD :].astype(jnp.bfloat16)
        return carry

    lax.fori_loop(0, LENGTH // 256, project, 0)

    def g_finish(j, carry):
        back = lax.rem(me.s + N_SEQ - j, N_SEQ)
        g_copy(j, back, back).wait_recv()
        g_copy(j, lax.rem(me.s + j, N_SEQ), me.s).wait_send()
        return carry

    lax.fori_loop(1, N_SEQ, g_finish, 0)
    for i in range(len(GATHER)):
        direction, rel, first, count, _ = GATHER[i]
        piece = part(rel, first, count)
        remote(piece, piece, x_send.at[i], x_recv.at[i], me.to(direction)).wait_send()
    for i in range(len(GATHER) + 1):
        core_copy(i).wait_send()
    save.wait()


NT = (((1,), (1,)), ((), ()))
TN = (((0,), (0,)), ((), ()))
QB = 256


def attention_kernel(b_ref, q_ref, k_ref, v_ref, g_ref, cos_ref, sin_ref, out_ref, sc, dp_sc, dk_sc, dv_sc, kt_sc):
    start = b_ref[0]
    kt_sc[...] = k_ref[...].T
    for i in range(LENGTH // QB):
        rows_i = pl.ds(i * QB, QB)
        q = q_ref[rows_i, :]
        g = g_ref[rows_i, :]
        q_pos = i * QB + lax.broadcasted_iota(jnp.int32, (1, QB), 1)
        low = jnp.where(q_pos < start, 0, start)
        top = jnp.full((1, QB), -1e30, jnp.float32)
        for j in range(i + 1):
            at = pl.ds(j * QB, QB)
            s = lax.dot_general(k_ref[at, :], q, NT, preferred_element_type=jnp.float32)
            k_pos = j * QB + lax.broadcasted_iota(jnp.int32, (QB, QB), 0)
            ok = k_pos >= low
            if j == i:
                ok = ok & (k_pos <= q_pos)
            s = jnp.where(ok, s, -1e30)
            sc[at, :] = s
            top = jnp.maximum(top, jnp.max(s, axis=0, keepdims=True))
        top = top * EXP2_SCALE
        total = jnp.zeros((1, QB), jnp.float32)
        for j in range(i + 1):
            at = pl.ds(j * QB, QB)
            e = jnp.exp2(sc[at, :] * EXP2_SCALE - top)
            sc[at, :] = e
            total = total + jnp.sum(e, axis=0, keepdims=True)
        inverse = 1.0 / total
        delta = jnp.zeros((1, QB), jnp.float32)
        for j in range(i + 1):
            at = pl.ds(j * QB, QB)
            p = sc[at, :] * inverse
            sc[at, :] = p
            low_p = p.astype(jnp.bfloat16)
            d = lax.dot_general(v_ref[at, :], g, NT, preferred_element_type=jnp.float32)
            dp_sc[at, :] = d
            delta = delta + jnp.sum(low_p.astype(jnp.float32) * d, axis=0, keepdims=True)
            dv = jnp.dot(low_p, g, preferred_element_type=jnp.float32)
            if j == i:
                dv_sc[at, :] = dv
            else:
                dv_sc[at, :] += dv
        dq = jnp.zeros((HEAD, QB), jnp.float32)
        for j in range(i + 1):
            at = pl.ds(j * QB, QB)
            ds = (sc[at, :] * (dp_sc[at, :] - delta)).astype(jnp.bfloat16)
            dk = jnp.dot(ds, q, preferred_element_type=jnp.float32)
            if j == i:
                dk_sc[at, :] = dk
            else:
                dk_sc[at, :] += dk
            dq = dq + jnp.dot(kt_sc[:, at], ds, preferred_element_type=jnp.float32)
        dq = dq.T * SCALE
        out_ref[rows_i, :HEAD] = (
            dq * cos_ref[rows_i, :] - pltpu.roll(dq, HEAD // 2, 1) * sin_ref[rows_i, :]
        ).astype(jnp.bfloat16)

    def finish(c, carry):
        at = pl.ds(pl.multiple_of(c * QB, QB), QB)
        dk = dk_sc[at, :] * SCALE
        out_ref[at, HEAD : 2 * HEAD] = (
            dk * cos_ref[at, :] - pltpu.roll(dk, HEAD // 2, 1) * sin_ref[at, :]
        ).astype(jnp.bfloat16)
        out_ref[at, 2 * HEAD :] = dv_sc[at, :].astype(jnp.bfloat16)
        return carry

    lax.fori_loop(0, LENGTH // QB, finish, 0)


ORDER = ((2, 1), (-1, 1), (1, 1), (2, 0), (0, 1), (-1, 0), (1, 0), (0, 0))
SLOT = {rel: n for n, rel in enumerate(ORDER)}
RECV_AT = []
_at = 0
for _piece in REDUCE:
    RECV_AT.append(_at)
    _at += _piece[3]
RECV_ROWS = _at


def scatter_kernel(
    g_ref, w_ref, rows_hbm,
    in_ref, dq_ref, dk_ref, dv_ref,
    rows, mine, away, near, arrived, dwt, kv_near, lo_in, z_in, kv_all,
    r_send, r_recv, n_send, n_recv, kv_sem, lo_sem, z_send, z_recv, a_send, a_recv, l_sem,
):
    me = Place()
    load = pltpu.make_async_copy(rows_hbm, rows, l_sem.at[0])
    load.start()
    enter(me, True)

    def partial_sum(rel, other_core):
        at = pl.ds(pl.multiple_of(me.block(rel, other_core) * ROWS, ROWS), ROWS)
        return lax.dot_general(
            g_ref[at, :], w_ref[...], NT, preferred_element_type=jnp.float32
        ).astype(jnp.bfloat16)

    def near_copy(n):
        return remote(away.at[n], near.at[n], n_send.at[n], n_recv.at[n], me.to("core"))

    def block_out(rel):
        n = SLOT[rel]
        away[n] = partial_sum(rel, 1)
        near_copy(n).start()
        mine[n] = partial_sum(rel, 0)

    def block_in(rel):
        n = SLOT[rel]
        near_copy(n).wait_recv()
        mine[n] = (mine[n].astype(jnp.float32) + near[n].astype(jnp.float32)).astype(jnp.bfloat16)

    def r_copy(i):
        direction, rel, first, count, _ = REDUCE[i]
        return remote(
            mine.at[SLOT[rel], pl.ds(first, count), :],
            arrived.at[pl.ds(RECV_AT[i], count), :],
            r_send.at[i],
            r_recv.at[i],
            me.to(direction),
        )

    def r_add(i):
        _, _, first, count, rel = REDUCE[i]
        r_copy(i).wait_recv()
        n = SLOT[rel]
        mine[n, pl.ds(first, count), :] = (
            mine[n, pl.ds(first, count), :].astype(jnp.float32)
            + arrived[pl.ds(RECV_AT[i], count), :].astype(jnp.float32)
        ).astype(jnp.bfloat16)

    block_out((2, 1))
    block_out((-1, 1))
    block_in((2, 1))
    for i in (0, 1, 2):
        r_copy(i).start()
    load.wait()

    kv_row = pl.multiple_of(HEAD + me.core * HEAD, HEAD)
    kv_other = pl.multiple_of(HEAD + (1 - me.core) * HEAD, HEAD)
    q_rows = pl.ds(0, HEAD)

    def weights(c, carry):
        at = pl.ds(pl.multiple_of(c * 512, 512), 512)
        dwt[:, at] = lax.dot_general(
            g_ref[...], rows[:, at], TN, preferred_element_type=jnp.float32
        ).astype(jnp.bfloat16)
        return carry

    lax.fori_loop(0, FEATURES // 512, weights, 0)
    kv_copy = remote(dwt.at[pl.ds(kv_other, HEAD), :], kv_near, kv_sem.at[0], kv_sem.at[1], me.to("core"))
    kv_copy.start()
    block_out((1, 1))
    block_out((2, 0))
    kv_copy.wait_recv()
    kv_rows = pl.ds(kv_row, HEAD)
    dwt[kv_rows, :] = (
        dwt[kv_rows, :].astype(jnp.float32) + kv_near[...].astype(jnp.float32)
    ).astype(jnp.bfloat16)

    half = N_FSDP // 2 * ROWS
    away_cols = pl.ds(pl.multiple_of((1 - me.lo) * half, half), half)
    own_cols = pl.ds(pl.multiple_of(me.lo * half, half), half)
    lo_device = ((1 - me.lo) * 8 + me.z, me.s)
    lo_q = remote(dwt.at[q_rows, away_cols], lo_in.at[0], lo_sem.at[0], lo_sem.at[1], lo_device)
    lo_kv = remote(dwt.at[kv_rows, away_cols], lo_in.at[1], lo_sem.at[2], lo_sem.at[3], lo_device)
    lo_q.start()
    lo_kv.start()

    block_in((-1, 1))
    r_add(0)
    r_copy(3).start()
    r_copy(5).start()
    block_in((1, 1))
    r_add(1)
    r_copy(4).start()
    r_copy(6).start()
    block_in((2, 0))
    r_add(2)
    r_copy(7).start()
    r_copy(8).start()
    block_out((0, 1))
    block_out((-1, 0))
    block_out((1, 0))
    block_out((0, 0))

    lo_q.wait_recv()
    lo_kv.wait_recv()
    lo_q.wait_send()
    lo_kv.wait_send()
    dwt[q_rows, own_cols] = (
        dwt[q_rows, own_cols].astype(jnp.float32) + lo_in[0].astype(jnp.float32)
    ).astype(jnp.bfloat16)
    dwt[kv_rows, own_cols] = (
        dwt[kv_rows, own_cols].astype(jnp.float32) + lo_in[1].astype(jnp.float32)
    ).astype(jnp.bfloat16)

    def z_copies(j, z_to):
        cols = pl.ds(pl.multiple_of((me.lo * 8 + z_to) * ROWS, ROWS), ROWS)
        device = (me.lo * 8 + z_to, me.s)
        return (
            remote(dwt.at[q_rows, cols], z_in.at[j, 0], z_send.at[0, j], z_recv.at[0, j], device),
            remote(dwt.at[kv_rows, cols], z_in.at[j, 1], z_send.at[1, j], z_recv.at[1, j], device),
        )

    def z_start(j, carry):
        for copy in z_copies(j, lax.rem(me.z + j, 8)):
            copy.start()
        return carry

    lax.fori_loop(1, 8, z_start, 0)

    block_in((0, 1))
    r_add(5)
    r_add(6)
    r_copy(9).start()
    block_in((-1, 0))
    r_add(3)
    r_add(7)
    r_copy(10).start()
    block_in((1, 0))
    r_add(4)
    r_add(8)
    r_copy(11).start()
    block_in((0, 0))

    own_piece = pl.ds(pl.multiple_of(me.f * ROWS, ROWS), ROWS)

    def z_add(j, sums):
        for copy in z_copies(j, lax.rem(me.z + j, 8)):
            copy.wait()
        return sums[0] + z_in[j, 0].astype(jnp.float32), sums[1] + z_in[j, 1].astype(jnp.float32)

    q_sum, kv_sum = lax.fori_loop(
        1,
        8,
        z_add,
        (dwt[q_rows, own_piece].astype(jnp.float32), dwt[kv_rows, own_piece].astype(jnp.float32)),
    )
    own_slot = kv_all.at[me.s]
    own_slot[...] = kv_sum.astype(jnp.bfloat16)

    def a_copy(j, source):
        return remote(
            kv_all.at[source],
            kv_all.at[source],
            a_send.at[j],
            a_recv.at[j],
            (me.f, lax.rem(me.s + j, N_SEQ)),
        )

    def a_start(j, carry):
        a_copy(j, me.s).start()
        return carry

    lax.fori_loop(1, N_SEQ, a_start, 0)
    dq_ref[...] = q_sum.T

    r_copy(9).wait_recv()
    r_copy(10).wait_recv()
    r_copy(11).wait_recv()
    n = SLOT[(0, 0)]
    total = mine[n].astype(jnp.float32)
    for i in (9, 10, 11):
        total = total + arrived[pl.ds(RECV_AT[i], ROWS), :].astype(jnp.float32)
    in_ref[...] = total.astype(jnp.bfloat16)

    def a_finish(j, carry):
        a_copy(j, lax.rem(me.s + N_SEQ - j, N_SEQ)).wait_recv()
        a_copy(j, me.s).wait_send()
        return carry

    lax.fori_loop(1, N_SEQ, a_finish, 0)
    for g in range(4):
        at = pl.ds(g * HEAD, HEAD)
        dk_ref[:, at] = (kv_all[4 * g].astype(jnp.float32) + kv_all[4 * g + 2].astype(jnp.float32)).T
        dv_ref[:, at] = (kv_all[4 * g + 1].astype(jnp.float32) + kv_all[4 * g + 3].astype(jnp.float32)).T

    kv_copy.wait_send()
    for i in range(len(REDUCE)):
        r_copy(i).wait_send()
    for n in range(len(ORDER)):
        near_copy(n).wait_send()


def rope_tables():
    half = HEAD // 2
    inverse = (500000.0 ** (-(np.arange(half, dtype=np.float64) * 2.0 / HEAD))).astype(np.float32)
    angles = np.arange(LENGTH, dtype=np.float32)[:, None] * inverse[None, :]
    cos, sin = np.cos(angles), np.sin(angles)
    return np.concatenate([cos, cos], axis=1), np.concatenate([-sin, sin], axis=1)


def vmem():
    return pl.BlockSpec(memory_space=pltpu.VMEM)


def shards(normed_input, out_grad, w_query, key_weight_matrix, value_weight_matrix, boundary):
    cos, sin = rope_tables()
    cos, sin = jnp.asarray(cos), jnp.asarray(sin)
    bf16, f32 = jnp.bfloat16, jnp.float32
    dma = pltpu.SemaphoreType.DMA
    shape = jax.ShapeDtypeStruct
    per_head = shape((LENGTH, HEAD), bf16)
    rows, q, k, v, g, w = pl.pallas_call(
        gather_kernel,
        out_shape=(shape((LENGTH, FEATURES), bf16), per_head, per_head, per_head, per_head, shape((FEATURES, 3 * HEAD), bf16)),
        in_specs=[vmem()] * 7,
        out_specs=(pl.BlockSpec(memory_space=pl.ANY),) + (vmem(),) * 5,
        scratch_shapes=[
            pltpu.VMEM((LENGTH, FEATURES), bf16),
            pltpu.VMEM((ROWS, HEAD), bf16),
            dma((len(GATHER),)),
            dma((len(GATHER),)),
            dma((len(GATHER) + 1,)),
            dma((len(GATHER) + 1,)),
            dma((N_SEQ,)),
            dma((N_SEQ,)),
            dma((2, N_FSDP)),
            dma((2, N_FSDP)),
            dma((1,)),
        ],
        compiler_params=pltpu.CompilerParams(collective_id=1, has_side_effects=True, vmem_limit_bytes=40 * 2**20),
        name="gather_project",
    )(normed_input[0], out_grad[0], w_query, key_weight_matrix, value_weight_matrix, cos, sin)

    grads = pl.pallas_call(
        attention_kernel,
        out_shape=shape((LENGTH, 3 * HEAD), bf16),
        in_specs=[pl.BlockSpec(memory_space=pltpu.SMEM)] + [vmem()] * 6,
        out_specs=vmem(),
        scratch_shapes=[
            pltpu.VMEM((LENGTH, QB), f32),
            pltpu.VMEM((LENGTH, QB), f32),
            pltpu.VMEM((LENGTH, HEAD), f32),
            pltpu.VMEM((LENGTH, HEAD), f32),
            pltpu.VMEM((HEAD, LENGTH), bf16),
        ],
        compiler_params=pltpu.CompilerParams(vmem_limit_bytes=40 * 2**20),
        name="attention_grads",
    )(boundary, q, k, v, g, cos, sin)

    input_grad, dq, dk, dv = pl.pallas_call(
        scatter_kernel,
        out_shape=(
            shape((ROWS, FEATURES), bf16),
            shape((ROWS, HEAD), f32),
            shape((ROWS, GROUP * HEAD), f32),
            shape((ROWS, GROUP * HEAD), f32),
        ),
        in_specs=[vmem(), vmem(), pl.BlockSpec(memory_space=pl.ANY)],
        out_specs=(vmem(),) * 4,
        scratch_shapes=[
            pltpu.VMEM((LENGTH, FEATURES), bf16),
            pltpu.VMEM((8, ROWS, FEATURES), bf16),
            pltpu.VMEM((8, ROWS, FEATURES), bf16),
            pltpu.VMEM((8, ROWS, FEATURES), bf16),
            pltpu.VMEM((RECV_ROWS, FEATURES), bf16),
            pltpu.VMEM((3 * HEAD, FEATURES), bf16),
            pltpu.VMEM((HEAD, FEATURES), bf16),
            pltpu.VMEM((2, HEAD, FEATURES // 2), bf16),
            pltpu.VMEM((8, 2, HEAD, ROWS), bf16),
            pltpu.VMEM((N_SEQ, HEAD, ROWS), bf16),
            dma((len(REDUCE),)),
            dma((len(REDUCE),)),
            dma((len(ORDER),)),
            dma((len(ORDER),)),
            dma((2,)),
            dma((4,)),
            dma((2, 8)),
            dma((2, 8)),
            dma((N_SEQ,)),
            dma((N_SEQ,)),
            dma((1,)),
        ],
        compiler_params=pltpu.CompilerParams(collective_id=2, has_side_effects=True, vmem_limit_bytes=48 * 2**20),
        name="scatter_grads",
    )(grads, w, rows)
    return (input_grad[None], dq, dk, dv)


def solution(mesh):
    return jax.shard_map(
        shards,
        mesh=mesh,
        in_specs=(
            P("fsdp", "seq", None),
            P("fsdp", "seq", None),
            P("fsdp", "seq"),
            P("fsdp", None),
            P("fsdp", None),
            P("fsdp"),
        ),
        out_specs=(P("fsdp", "seq", None), P("fsdp", "seq"), P("fsdp", None), P("fsdp", None)),
        check_vma=False,
    )
```

time: 647 us -> 146 us (0.23)
  waiting for transfers between devices: 469 us -> 0 us
  Pallas kernels: 0 us -> 134 us
  blocking collectives: 87.5 us -> 0 us
  matrix products: 33.3 us -> 0 us
  other arithmetic: 19.1 us -> 0 us
  between operations: 15.4 us -> 1.34 us
  starting transfers between devices: 8.95 us -> 0 us
    reduce_scatter x3 -> x0, waiting for transfers between devices: 259 us -> none  [the longest x1 112 us: shards(): lax.psum_scatter(lax.dot_general(grad_cols, wide_weights, (((1,), (1,)),...]
    psum x1 -> x0, waiting for transfers between devices: 151 us -> none  [shards(): lax.psum(key_part.astype(jnp.bfloat16), 'seq').astype(jnp.float32)]
    pallas_call x0 -> x3, Pallas kernels: none -> 134 us  [the longest x1 64.5 us: shards(): pl.pallas_call(gather_kernel, out_shape=(shape((LENGTH, FEATURES), bf16),...]
    all_gather x3 -> x0, blocking collectives: 87.5 us -> none  [the longest x1 32.4 us: shards(): lax.all_gather(w_query, 'fsdp', axis=0, tiled=True)]
    unnamed x7 -> x0, waiting for transfers between devices: 59 us -> none
    dot_general x27 -> x0, matrix products: 33.3 us -> none  [the longest x1 9.69 us: shards(): lax.dot_general(grad_cols, wide_weights, (((1,), (1,)), ((), ())), prefer...]
    unnamed x5 -> x0, other arithmetic: 9.25 us -> none
    all_to_all x1 -> x0, starting transfers between devices: 8.45 us -> none  [shards(): lax.all_to_all(grad_split, 'seq', split_axis=1, concat_axis=0, tiled=True)]
  transfers between devices with their start and end apart: 7 -> 0, of which waited for: 5 -> 0; matrix products, arithmetic and copies ran while one was open for 3% -> 0% of each run, Pallas kernels for 0% -> 0%
where the time goes in v1:
time: 146 us
  Pallas kernels  134 us (92%)
  local copies, waits for them, and re-layouts  9.93 us (7%)
    pallas_call x1, Pallas kernels, shards(): pl.pallas_call(gather_kernel, out_shape=(shape((LENGTH, FEATURES), bf16),...  64.5 us
    pallas_call x1, Pallas kernels, shards(): pl.pallas_call(scatter_kernel, out_shape=(shape((ROWS, FEATURES), bf16),...  59.7 us
    pallas_call x1, Pallas kernels, shards(): pl.pallas_call(attention_kernel, out_shape=shape((LENGTH, 3 * HEAD), bf16...  10.1 us
    unnamed x22, local copies, waits for them, and re-layouts  9.93 us

profile of v1, /device:TPU:1, one launch (start us, length us, event | category | flops | bytes accessed | tf_op | source)
XLA Modules:
  0.0 145.6 jit_solution(8746937457973961398)
XLA Ops:
  1.3 0.0 copy-start
  1.3 1.2 copy-done
  2.5 0.0 copy-start.2
  2.5 1.2 copy-done.2
  3.7 0.0 copy-start.4
  3.7 1.0 copy-done.4
  4.8 0.0 copy-start.5
  4.8 1.0 copy-done.5
  5.8 0.0 copy-start.6
  5.8 0.9 copy-done.6
  6.7 0.0 copy-start.7
  6.7 0.9 copy-done.7
  7.6 0.0 copy-start.8
  7.6 0.8 copy-done.8
  8.4 0.0 copy-start.1
  8.4 0.0 copy-start.3
  8.4 64.5 %gather_project.1 = (bf16[2048,2048]{1,0:T(8,128)(2,1)}, bf16[2048,128]{1,0:T(8,128)(2,1)S(1)}, bf16[2048,128]{1,0:T(8,128)(2,1)S(1)}, bf16[2048,128]{1,0:T(8,12...) custom-call(bf16[128,2048]{1,0:T(8,128)(2,1)S(1)} %bitcast.4, bf16[128,2048]{1,0:T(8,128)(2,1)S(1)} %bitcast.5, ...), custom_call_target="tpu_custom_call" | custom-call | tf_op jit(solution)/shard_map/gather_project/pallas_call | solution.py:576
  72.9 0.0 copy-done.1
  72.9 0.0 copy-done.3
  72.9 10.1 %attention_grads.1.g_ref = bf16[2048,384]{1,0:T(8,128)(2,1)S(1)} custom-call(s32[1]{0:T(128)S(6)} %copy.16.b_ref, bf16[2048,128]{1,0:T(8,128)(2,1)S(1)} %get-tuple-element.14.q_ref, bf16[2048,128]{1,0:T(8,128)(2,1)S(1)} %get-tuple-element.15.k_ref, bf16[2048,128]{1,0:T(8,128)(2,1)S(1)} %get-tuple-element.16.v_ref, ...), custom_call_target="tpu_custom_call" | custom-call | tf_op jit(solution)/shard_map/attention_grads/pallas_call | solution.py:598
  83.1 59.7 %scatter_grads.1 = (bf16[128,2048]{1,0:T(8,128)(2,1)S(1)}, f32[128,128]{1,0:T(8,128)S(1)}, f32[128,512]{1,0:T(8,128)S(1)}, f32[128,512]{1,0:T(8,128)S(1)}) custom-call(bf16[2048,384]{1,0:T(8,128)(2,1)S(1)} %attention_grads.1.g_ref, bf16[2048,384]{1,0:T(8,128)(2,1)S(1)} %get-tuple-element.18.w_ref, bf16[2048,2048]{1,0:T(8,128)(2,1)} %get-tuple-element.19.rows_hbm), custom_call_target="tpu_custom_call" | custom-call | tf_op jit(solution)/shard_map/scatter_grads/pallas_call | solution.py:614
  142.8 0.8 copy.17
  143.6 0.6 copy.18
  144.2 0.7 copy.19
  144.9 0.7 copy.20
Async XLA Ops:
  1.3 1.2 copy-start
  2.5 1.2 copy-start.2
  3.7 1.0 copy-start.4
  4.8 1.0 copy-start.5
  5.8 0.9 copy-start.6
  6.7 0.9 copy-start.7
  7.6 0.8 copy-start.8
  8.4 64.5 %copy-start.1 = (f32[2048,128]{1,0:T(8,128)S(1)}, f32[2048,128]{1,0:T(8,128)}, u32[]{:S(2)}) copy-start(f32[2048,128]{1,0:T(8,128)} %constant.5.clone.sin_ref) | copy-start | bytes 3145732
  8.4 64.5 %copy-start.3 = (f32[2048,128]{1,0:T(8,128)S(1)}, f32[2048,128]{1,0:T(8,128)}, u32[]{:S(2)}) copy-start(f32[2048,128]{1,0:T(8,128)} %constant.4.clone.cos_ref) | copy-start | bytes 3145732

commit v2 on v1

v2 whole, which is shorter than its diff:
```python
import jax
import jax.numpy as jnp
import numpy as np
from jax import lax
from jax.experimental import pallas as pl
from jax.experimental.pallas import tpu as pltpu
from jax.sharding import PartitionSpec as P

HEAD = 128
N_SEQ = 16
N_FSDP = 16
ROWS = 128
LENGTH = 2048
FEATURES = 2048
GROUP = 4
MESH = pl.DeviceIdType.MESH
SCALE = HEAD ** (-0.5)
EXP2_SCALE = SCALE * 1.4426950408889634

GATHER = (
    ("up", (0, 0), 0, 64, (-1, 0)),
    ("down", (0, 0), 64, 64, (1, 0)),
    ("side", (0, 0), 0, 64, (0, 1)),
    ("up", (0, 0), 64, 64, (-1, 0)),
    ("down", (0, 0), 0, 64, (1, 0)),
    ("side", (0, 0), 64, 64, (0, 1)),
    ("up", (-1, 0), 0, 64, (2, 0)),
    ("down", (1, 0), 64, 64, (2, 0)),
    ("side", (-1, 0), 0, 64, (-1, 1)),
    ("side", (1, 0), 64, 64, (1, 1)),
    ("down", (0, 1), 0, 64, (1, 1)),
    ("up", (0, 1), 64, 64, (-1, 1)),
    ("up", (-1, 1), 0, 48, (2, 1)),
    ("down", (1, 1), 80, 48, (2, 1)),
    ("side", (2, 0), 48, 32, (2, 1)),
)

REDUCE = (
    ("down", (2, 1), 0, 48, (-1, 1)),
    ("up", (2, 1), 80, 48, (1, 1)),
    ("side", (2, 1), 48, 32, (2, 0)),
    ("down", (-1, 1), 64, 64, (0, 1)),
    ("up", (1, 1), 0, 64, (0, 1)),
    ("side", (-1, 1), 0, 64, (-1, 0)),
    ("side", (1, 1), 64, 64, (1, 0)),
    ("down", (2, 0), 0, 64, (-1, 0)),
    ("up", (2, 0), 64, 64, (1, 0)),
    ("down", (-1, 0), 64, 64, (0, 0)),
    ("up", (1, 0), 0, 64, (0, 0)),
    ("side", (0, 1), 0, 64, (0, 0)),
    ("side", (0, 1), 64, 64, (0, 0)),
    ("down", (-1, 0), 0, 64, (0, 0)),
    ("up", (1, 0), 64, 64, (0, 0)),
)
LAST = ((0, (10, 11, 13)), (64, (9, 12, 14)))


class Place:
    def __init__(self):
        self.f = lax.axis_index("fsdp")
        self.s = lax.axis_index("seq")
        self.core = lax.rem(self.s, 2)
        self.hi = lax.rem(lax.div(self.s, 2), 2)
        self.y = lax.div(self.s, 4)
        self.z = lax.rem(self.f, 8)
        self.lo = lax.div(self.f, 8)

    def to(self, direction):
        s = self.s
        if direction == "up":
            return (self.f, lax.rem(s + 4, N_SEQ))
        if direction == "down":
            return (self.f, lax.rem(s + 12, N_SEQ))
        if direction == "side":
            return (self.f, s + 2 - 4 * self.hi)
        if direction == "lo":
            return ((1 - self.lo) * 8 + self.z, s)
        return (self.f, s + 1 - 2 * self.core)

    def block(self, rel, other_core=0):
        dy, dh = rel
        y = lax.rem(self.y + dy + 4, 4)
        hi = 1 - self.hi if dh else self.hi
        core = 1 - self.core if other_core else self.core
        return y * 4 + hi * 2 + core


def enter(me):
    barrier = pltpu.get_barrier_semaphore()

    def greet(j, carry):
        for device in ((me.f, lax.rem(me.s + j, N_SEQ)), (lax.rem(me.f + j, N_FSDP), me.s)):
            pl.semaphore_signal(barrier, inc=1, device_id=device, device_id_type=MESH)
        return carry

    lax.fori_loop(1, N_SEQ, greet, 0)
    pl.semaphore_wait(barrier, 2 * (N_SEQ - 1))


def remote(src, dst, send, recv, device):
    return pltpu.make_async_remote_copy(
        src_ref=src,
        dst_ref=dst,
        send_sem=send,
        recv_sem=recv,
        device_id=device,
        device_id_type=MESH,
    )


CHIP_PARTS = (
    ((-1, 0), (0, 3)),
    ((1, 0), (1, 4)),
    ((0, 1), (2, 5)),
    ((2, 0), (6, 7)),
    ((-1, 1), (8, 11)),
    ((1, 1), (9, 10)),
    ((2, 1), (12, 13, 14)),
)


def gather(
    me, x_hbm, g_hbm, wq_hbm, wk_hbm, wv_hbm, cos_hbm, sin_hbm,
    rows, q_ref, k_ref, v_ref, grad_ref, w_ref,
    cos_ref, sin_ref, x_send, x_recv, c_send, c_recv, g_send, g_recv, w_send, w_recv, l_sem,
):
    own = pl.multiple_of(me.s * ROWS, ROWS)
    head_col = pl.multiple_of(me.y * HEAD, HEAD)
    own_w = pl.ds(pl.multiple_of(me.f * ROWS, ROWS), ROWS)
    loads = [
        pltpu.make_async_copy(wq_hbm, w_ref.at[own_w, pl.ds(0, HEAD)], l_sem.at[0]),
        pltpu.make_async_copy(wk_hbm.at[:, pl.ds(head_col, HEAD)], w_ref.at[own_w, pl.ds(HEAD, HEAD)], l_sem.at[1]),
        pltpu.make_async_copy(wv_hbm.at[:, pl.ds(head_col, HEAD)], w_ref.at[own_w, pl.ds(HEAD, HEAD)], l_sem.at[1]),
        pltpu.make_async_copy(x_hbm, rows.at[pl.ds(own, ROWS), :], l_sem.at[2]),
        pltpu.make_async_copy(cos_hbm, cos_ref, l_sem.at[3]),
        pltpu.make_async_copy(sin_hbm, sin_ref, l_sem.at[4]),
        pltpu.make_async_copy(g_hbm.at[:, pl.ds(own, HEAD)], grad_ref.at[pl.ds(own, ROWS), :], l_sem.at[5]),
    ]
    loads[0].start()

    @pl.when(me.core == 0)
    def _():
        loads[1].start()

    @pl.when(me.core == 1)
    def _():
        loads[2].start()

    for load in loads[3:]:
        load.start()

    enter(me)

    def w_piece(lo, z):
        at = pl.multiple_of((lo * 8 + z) * ROWS, ROWS)
        return w_ref.at[pl.ds(at, ROWS), pl.ds(0, 2 * HEAD)]

    def w_copy(lo, z, slot, device):
        piece = w_piece(lo, z)
        return remote(piece, piece, w_send.at[slot], w_recv.at[slot], device)

    def w_push(j, other):
        lo = 1 - me.lo if other else me.lo
        return w_copy(lo, me.z, 8 * other + j, (me.lo * 8 + lax.rem(me.z + j, 8), me.s))

    def w_start(other):
        def step(j, carry):
            w_push(j, other).start()
            return carry

        lax.fori_loop(1, 8, step, 0)

    def w_finish(j, carry):
        back = lax.rem(me.z + 8 - j, 8)
        for other in (0, 1):
            lo = 1 - me.lo if other else me.lo
            w_copy(lo, back, 8 * other + j, me.to("lo")).wait_recv()
        return carry

    def w_sent(j, carry):
        for other in (0, 1):
            w_push(j, other).wait_send()
        return carry

    def part(rel, first, count, other_core=0):
        at = pl.multiple_of(me.block(rel, other_core) * ROWS + first, 16)
        return rows.at[pl.ds(at, count), :]

    def x_copy(i):
        direction, rel, first, count, _ = GATHER[i]
        piece = part(rel, first, count)
        source = x_hbm.at[pl.ds(first, count), :] if rel == (0, 0) else piece
        return remote(source, piece, x_send.at[i], x_recv.at[i], me.to(direction))

    def x_start(i):
        x_copy(i).start()

    def x_arrived(i):
        direction, _, first, count, rel = GATHER[i]
        piece = part(rel, first, count)
        remote(piece, piece, x_send.at[i], x_recv.at[i], me.to(direction)).wait_recv()
        core_copy(i).start()

    def core_copy(i, receive=False):
        rel, first, count = (0, 0), 0, 128
        if i < len(GATHER):
            _, _, first, count, rel = GATHER[i]
        piece = part(rel, first, count, other_core=1 if receive else 0)
        source = x_hbm if rel == (0, 0) and not receive else piece
        return remote(source, piece, c_send.at[i], c_recv.at[i], me.to("core"))

    def g_copy(j, device_s, source_s):
        at = pl.multiple_of(source_s * ROWS, ROWS)
        col = pl.multiple_of(device_s * HEAD, HEAD)
        return remote(
            g_hbm.at[:, pl.ds(col, HEAD)],
            grad_ref.at[pl.ds(at, ROWS), :],
            g_send.at[j],
            g_recv.at[j],
            (me.f, device_s),
        )

    def g_start(j, carry):
        g_copy(j, lax.rem(me.s + j, N_SEQ), me.s).start()
        return carry

    def project(rel, parts):
        for i in parts:
            core_copy(i, True).wait_recv()
        hi = 1 - me.hi if rel[1] else me.hi
        chip = lax.rem(me.y + rel[0] + 4, 4) * 2 + hi
        at = pl.ds(pl.multiple_of(chip * 256, 256), 256)
        full = jnp.dot(rows[at, :], w_ref[...], preferred_element_type=jnp.float32)
        cos, sin = cos_ref[at, :], sin_ref[at, :]
        q, first, second = full[:, :HEAD], full[:, HEAD : 2 * HEAD], full[:, 2 * HEAD :]
        is_key = me.core == 0
        k, v = jnp.where(is_key, first, second), jnp.where(is_key, second, first)
        q_ref[at, :] = (q * cos + pltpu.roll(q, HEAD // 2, 1) * sin).astype(jnp.bfloat16)
        k_ref[at, :] = (k * cos + pltpu.roll(k, HEAD // 2, 1) * sin).astype(jnp.bfloat16)
        v_ref[at, :] = v.astype(jnp.bfloat16)

    for i in range(6):
        x_start(i)
    loads[0].wait()
    loads[1].wait()
    own_to_lo = w_copy(me.lo, me.z, 0, me.to("lo"))
    own_to_lo.start()
    w_start(0)
    core_copy(len(GATHER)).start()
    w_copy(1 - me.lo, me.z, 0, me.to("lo")).wait_recv()
    w_start(1)
    x_arrived(0)
    x_start(6)
    x_start(8)
    x_arrived(1)
    x_start(7)
    x_start(9)
    x_arrived(2)
    x_start(10)
    x_arrived(5)
    x_start(11)
    x_arrived(3)
    x_arrived(4)
    x_arrived(8)
    x_start(12)
    x_arrived(9)
    x_start(13)
    x_arrived(6)
    x_arrived(7)
    x_start(14)
    lax.fori_loop(1, N_SEQ, g_start, 0)
    for load in loads[3:]:
        load.wait()
    lax.fori_loop(1, 8, w_finish, 0)
    share = remote(
        w_ref.at[:, pl.ds(HEAD, HEAD)],
        w_ref.at[:, pl.ds(2 * HEAD, HEAD)],
        w_send.at[8],
        w_recv.at[8],
        me.to("core"),
    )
    share.start()
    share.wait_recv()
    project((0, 0), (len(GATHER),))
    for rel, parts in CHIP_PARTS[:4]:
        project(rel, parts)
    x_arrived(10)
    x_arrived(11)
    for rel, parts in CHIP_PARTS[4:6]:
        project(rel, parts)
    for i in CHIP_PARTS[6][1]:
        x_arrived(i)
    project(*CHIP_PARTS[6])

    def g_finish(j, carry):
        back = lax.rem(me.s + N_SEQ - j, N_SEQ)
        g_copy(j, back, back).wait_recv()
        g_copy(j, lax.rem(me.s + j, N_SEQ), me.s).wait_send()
        return carry

    lax.fori_loop(1, N_SEQ, g_finish, 0)
    share.wait_send()
    own_to_lo.wait_send()
    lax.fori_loop(1, 8, w_sent, 0)
    for i in range(len(GATHER)):
        x_copy(i).wait_send()
    for i in range(len(GATHER) + 1):
        core_copy(i).wait_send()


NT = (((1,), (1,)), ((), ()))
TN = (((0,), (0,)), ((), ()))
QB = 256


def attention(me, b_ref, q_ref, k_ref, v_ref, g_ref, cos_ref, sin_ref, out_ref, sc, dp_sc, dk_sc, dv_sc, kt_sc):
    start = b_ref[0]
    kt_sc[...] = k_ref[...].T
    for i in range(LENGTH // QB):
        rows_i = pl.ds(i * QB, QB)
        q = q_ref[rows_i, :]
        g = g_ref[rows_i, :]
        q_pos = i * QB + lax.broadcasted_iota(jnp.int32, (1, QB), 1)
        low = jnp.where(q_pos < start, 0, start)
        top = jnp.full((1, QB), -1e30, jnp.float32)
        for j in range(i + 1):
            at = pl.ds(j * QB, QB)
            s = lax.dot_general(k_ref[at, :], q, NT, preferred_element_type=jnp.float32)
            k_pos = j * QB + lax.broadcasted_iota(jnp.int32, (QB, QB), 0)
            ok = k_pos >= low
            if j == i:
                ok = ok & (k_pos <= q_pos)
            s = jnp.where(ok, s, -1e30)
            sc[at, :] = s
            top = jnp.maximum(top, jnp.max(s, axis=0, keepdims=True))
        top = top * EXP2_SCALE
        total = jnp.zeros((1, QB), jnp.float32)
        for j in range(i + 1):
            at = pl.ds(j * QB, QB)
            e = jnp.exp2(sc[at, :] * EXP2_SCALE - top)
            sc[at, :] = e
            total = total + jnp.sum(e, axis=0, keepdims=True)
        inverse = 1.0 / total
        delta = jnp.zeros((1, QB), jnp.float32)
        for j in range(i + 1):
            at = pl.ds(j * QB, QB)
            p = sc[at, :] * inverse
            sc[at, :] = p
            low_p = p.astype(jnp.bfloat16)
            d = lax.dot_general(v_ref[at, :], g, NT, preferred_element_type=jnp.float32)
            dp_sc[at, :] = d
            delta = delta + jnp.sum(low_p.astype(jnp.float32) * d, axis=0, keepdims=True)
            dv = jnp.dot(low_p, g, preferred_element_type=jnp.float32)
            if j == i:
                dv_sc[at, :] = dv
            else:
                dv_sc[at, :] += dv
        dq = jnp.zeros((HEAD, QB), jnp.float32)
        for j in range(i + 1):
            at = pl.ds(j * QB, QB)
            ds = (sc[at, :] * (dp_sc[at, :] - delta)).astype(jnp.bfloat16)
            dk = jnp.dot(ds, q, preferred_element_type=jnp.float32)
            if j == i:
                dk_sc[at, :] = dk
            else:
                dk_sc[at, :] += dk
            dq = dq + jnp.dot(kt_sc[:, at], ds, preferred_element_type=jnp.float32)
        dq = dq.T * SCALE
        out_ref[rows_i, :HEAD] = (
            dq * cos_ref[rows_i, :] - pltpu.roll(dq, HEAD // 2, 1) * sin_ref[rows_i, :]
        ).astype(jnp.bfloat16)

    key_col = pl.ds(pl.multiple_of(HEAD + me.core * HEAD, HEAD), HEAD)
    value_col = pl.ds(pl.multiple_of(2 * HEAD - me.core * HEAD, HEAD), HEAD)

    def finish(c, carry):
        at = pl.ds(pl.multiple_of(c * QB, QB), QB)
        dk = dk_sc[at, :] * SCALE
        out_ref[at, key_col] = (
            dk * cos_ref[at, :] - pltpu.roll(dk, HEAD // 2, 1) * sin_ref[at, :]
        ).astype(jnp.bfloat16)
        out_ref[at, value_col] = dv_sc[at, :].astype(jnp.bfloat16)
        return carry

    lax.fori_loop(0, LENGTH // QB, finish, 0)


ORDER = ((2, 1), (-1, 1), (1, 1), (2, 0), (0, 1), (-1, 0), (1, 0), (0, 0))
SLOT = {rel: n for n, rel in enumerate(ORDER)}
RECV_AT = []
_at = 0
for _piece in REDUCE:
    RECV_AT.append(_at)
    _at += _piece[3]
RECV_ROWS = _at


def scatter(
    me, g_ref, w_ref, rows, in_ref, dq_ref, dk_ref, dv_ref,
    mine, away, near, arrived, dwq, dwm, dwo, kv_near, f_in, kv_all,
    r_send, r_recv, n_send, n_recv, kv_sem, f_send, f_recv, a_send, a_recv,
):
    def partial_sum(rel, other_core):
        at = pl.ds(pl.multiple_of(me.block(rel, other_core) * ROWS, ROWS), ROWS)
        return lax.dot_general(
            g_ref[at, :], w_ref[...], NT, preferred_element_type=jnp.float32
        ).astype(jnp.bfloat16)

    def near_copy(n):
        return remote(away.at[n], near.at[n], n_send.at[n], n_recv.at[n], me.to("core"))

    def block_out(rel):
        n = SLOT[rel]
        away[n] = partial_sum(rel, 1)
        near_copy(n).start()
        mine[n] = partial_sum(rel, 0)

    def block_in(rel):
        n = SLOT[rel]
        near_copy(n).wait_recv()
        mine[n] = (mine[n].astype(jnp.float32) + near[n].astype(jnp.float32)).astype(jnp.bfloat16)

    def r_copy(i):
        direction, rel, first, count, _ = REDUCE[i]
        return remote(
            mine.at[SLOT[rel], pl.ds(first, count), :],
            arrived.at[pl.ds(RECV_AT[i], count), :],
            r_send.at[i],
            r_recv.at[i],
            me.to(direction),
        )

    def r_add(i):
        _, _, first, count, rel = REDUCE[i]
        r_copy(i).wait_recv()
        n = SLOT[rel]
        mine[n, pl.ds(first, count), :] = (
            mine[n, pl.ds(first, count), :].astype(jnp.float32)
            + arrived[pl.ds(RECV_AT[i], count), :].astype(jnp.float32)
        ).astype(jnp.bfloat16)

    def weights(first_col, count, targets):
        def step(c, carry):
            at = pl.ds(pl.multiple_of(c * 512, 512), 512)
            part = lax.dot_general(
                g_ref[:, pl.ds(first_col, count)], rows[:, at], TN, preferred_element_type=jnp.float32
            ).astype(jnp.bfloat16)
            for n, target in enumerate(targets):
                for k in range(4):
                    target[c * 4 + k] = part[n * HEAD : (n + 1) * HEAD, k * ROWS : (k + 1) * ROWS]
            return carry

        lax.fori_loop(0, FEATURES // 512, step, 0)

    kv_copy = remote(dwo, kv_near, kv_sem.at[0], kv_sem.at[1], me.to("core"))

    def f_copy(source, kind, j):
        to = lax.rem(me.f + j, N_FSDP)
        return remote(source.at[to], f_in.at[kind, j], f_send.at[kind, j], f_recv.at[kind, j], (to, me.s))

    def f_start(source, kind):
        def step(j, carry):
            f_copy(source, kind, j).start()
            return carry

        lax.fori_loop(1, N_FSDP, step, 0)

    def f_sum(source, kind):
        def step(j, total):
            f_copy(source, kind, j).wait()
            return total + f_in[kind, j].astype(jnp.float32)

        return lax.fori_loop(1, N_FSDP, step, source[me.f].astype(jnp.float32))

    chip = lax.div(me.s, 2)

    def a_copy(j, source):
        slot = kv_all.at[me.core, source]
        to = (me.f, lax.rem(me.s + 2 * j, N_SEQ))
        return remote(slot, slot, a_send.at[j], a_recv.at[j], to)

    def a_start(j, carry):
        a_copy(j, chip).start()
        return carry

    def a_arrived(j, carry):
        a_copy(j, lax.rem(chip + 8 - j, 8)).wait_recv()
        return carry

    def a_sent(j, carry):
        a_copy(j, chip).wait_send()
        return carry

    def r_start(*pieces):
        for i in pieces:
            r_copy(i).start()

    block_out((2, 1))
    block_out((-1, 1))
    block_in((2, 1))
    r_start(0, 1, 2)
    block_out((1, 1))
    block_in((-1, 1))
    r_start(3)
    weights(HEAD, 2 * HEAD, (dwm, dwo))
    kv_copy.start()
    block_in((1, 1))
    r_start(4)
    block_out((2, 0))
    weights(0, HEAD, (dwq,))
    f_start(dwq, 0)
    kv_copy.wait_recv()

    def kv_add(c, carry):
        dwm[c] = (dwm[c].astype(jnp.float32) + kv_near[c].astype(jnp.float32)).astype(jnp.bfloat16)
        return carry

    lax.fori_loop(0, N_FSDP, kv_add, 0)
    f_start(dwm, 1)
    r_add(0)
    r_start(5)
    r_add(1)
    r_start(6)
    block_in((2, 0))
    r_add(2)
    r_start(7, 8)
    block_out((-1, 0))
    block_out((1, 0))
    block_in((-1, 0))
    r_start(9)
    block_in((1, 0))
    r_start(10)
    block_out((0, 1))
    block_out((0, 0))
    block_in((0, 1))
    r_add(3)
    r_add(4)
    r_start(11, 12)
    block_in((0, 0))
    r_add(5)
    r_add(7)
    r_start(13)
    r_add(6)
    r_add(8)
    r_start(14)
    kv_all[me.core, chip] = f_sum(dwm, 1).astype(jnp.bfloat16)
    lax.fori_loop(1, 8, a_start, 0)
    dq_ref[...] = f_sum(dwq, 0).T
    lax.fori_loop(1, 8, a_arrived, 0)
    kv_mine, kv_theirs = kv_all.at[me.core], kv_all.at[1 - me.core]
    kv_share = remote(kv_mine, kv_mine, kv_sem.at[2], kv_sem.at[3], me.to("core"))
    kv_share.start()
    for first, pieces in LAST:
        total = mine[SLOT[(0, 0)], pl.ds(first, 64), :].astype(jnp.float32)
        for i in pieces:
            r_copy(i).wait_recv()
            total = total + arrived[pl.ds(RECV_AT[i], 64), :].astype(jnp.float32)
        in_ref[pl.ds(first, 64), :] = total.astype(jnp.bfloat16)
    remote(kv_theirs, kv_theirs, kv_sem.at[2], kv_sem.at[3], me.to("core")).wait_recv()
    for n in range(4):
        at = pl.ds(n * HEAD, HEAD)
        for kind, out in ((0, dk_ref), (1, dv_ref)):
            out[:, at] = (
                kv_all[kind, 2 * n].astype(jnp.float32) + kv_all[kind, 2 * n + 1].astype(jnp.float32)
            ).T
    lax.fori_loop(1, 8, a_sent, 0)
    kv_share.wait_send()
    kv_copy.wait_send()
    for i in range(len(REDUCE)):
        r_copy(i).wait_send()
    for n in range(len(ORDER)):
        near_copy(n).wait_send()


def whole_kernel(
    x_hbm, g_hbm, wq_hbm, wk_hbm, wv_hbm, cos_hbm, sin_hbm, b_ref,
    in_ref, dq_ref, dk_ref, dv_ref,
    rows, q_ref, k_ref, v_ref, grad_ref, w_ref, cos_ref, sin_ref,
    sc, dp_sc, dk_sc, dv_sc, kt_sc, cols,
    mine, away, near, arrived, dwq, dwm, dwo, kv_near, f_in, kv_all,
    *sems,
):
    me = Place()
    gather(
        me, x_hbm, g_hbm, wq_hbm, wk_hbm, wv_hbm, cos_hbm, sin_hbm,
        rows, q_ref, k_ref, v_ref, grad_ref, w_ref, cos_ref, sin_ref, *sems[:9],
    )
    attention(me, b_ref, q_ref, k_ref, v_ref, grad_ref, cos_ref, sin_ref, cols, sc, dp_sc, dk_sc, dv_sc, kt_sc)
    scatter(
        me, cols, w_ref, rows, in_ref, dq_ref, dk_ref, dv_ref,
        mine, away, near, arrived, dwq, dwm, dwo, kv_near, f_in, kv_all, *sems[9:],
    )


def rope_tables():
    half = HEAD // 2
    inverse = (500000.0 ** (-(np.arange(half, dtype=np.float64) * 2.0 / HEAD))).astype(np.float32)
    angles = np.arange(LENGTH, dtype=np.float32)[:, None] * inverse[None, :]
    cos, sin = np.cos(angles), np.sin(angles)
    return np.concatenate([cos, cos], axis=1), np.concatenate([-sin, sin], axis=1)


def vmem():
    return pl.BlockSpec(memory_space=pltpu.VMEM)


BF16, F32 = jnp.bfloat16, jnp.float32
dma = pltpu.SemaphoreType.DMA
shape = jax.ShapeDtypeStruct
VMEM_LIMIT = 62 * 2**20


def run(x, g, wq, wk, wv, cos, sin, boundary):
    per_head = pltpu.VMEM((LENGTH, HEAD), BF16)
    table = pltpu.VMEM((LENGTH, HEAD), F32)
    scores = pltpu.VMEM((LENGTH, QB), F32)
    blocks = pltpu.VMEM((8, ROWS, FEATURES), BF16)
    pieces = pltpu.VMEM((N_FSDP, HEAD, ROWS), BF16)
    hbm = pl.BlockSpec(memory_space=pltpu.HBM)
    return pl.pallas_call(
        whole_kernel,
        out_shape=(
            shape((ROWS, FEATURES), BF16),
            shape((ROWS, HEAD), F32),
            shape((ROWS, GROUP * HEAD), F32),
            shape((ROWS, GROUP * HEAD), F32),
        ),
        in_specs=[hbm] * 7 + [pl.BlockSpec(memory_space=pltpu.SMEM)],
        out_specs=(vmem(),) * 4,
        scratch_shapes=[
            pltpu.VMEM((LENGTH, FEATURES), BF16),
            per_head,
            per_head,
            per_head,
            per_head,
            pltpu.VMEM((FEATURES, 3 * HEAD), BF16),
            table,
            table,
            scores,
            scores,
            table,
            table,
            pltpu.VMEM((HEAD, LENGTH), BF16),
            pltpu.VMEM((LENGTH, 3 * HEAD), BF16),
            blocks,
            blocks,
            blocks,
            pltpu.VMEM((RECV_ROWS, FEATURES), BF16),
            pieces,
            pieces,
            pieces,
            pieces,
            pltpu.VMEM((2, N_FSDP, HEAD, ROWS), BF16),
            pltpu.VMEM((2, 8, HEAD, ROWS), BF16),
            dma((len(GATHER),)),
            dma((len(GATHER),)),
            dma((len(GATHER) + 1,)),
            dma((len(GATHER) + 1,)),
            dma((N_SEQ,)),
            dma((N_SEQ,)),
            dma((16,)),
            dma((16,)),
            dma((6,)),
            dma((len(REDUCE),)),
            dma((len(REDUCE),)),
            dma((len(ORDER),)),
            dma((len(ORDER),)),
            dma((4,)),
            dma((2, N_FSDP)),
            dma((2, N_FSDP)),
            dma((8,)),
            dma((8,)),
        ],
        compiler_params=pltpu.CompilerParams(collective_id=1, has_side_effects=True, vmem_limit_bytes=VMEM_LIMIT),
        name="attention_backward",
    )(x, g, wq, wk, wv, cos, sin, boundary)


def shards(normed_input, out_grad, w_query, key_weight_matrix, value_weight_matrix, boundary):
    cos, sin = rope_tables()
    input_grad, dq, dk, dv = run(
        normed_input[0], out_grad[0], w_query, key_weight_matrix, value_weight_matrix,
        jnp.asarray(cos), jnp.asarray(sin), boundary,
    )
    return (input_grad[None], dq, dk, dv)


def solution(mesh):
    return jax.shard_map(
        shards,
        mesh=mesh,
        in_specs=(
            P("fsdp", "seq", None),
            P("fsdp", "seq", None),
            P("fsdp", "seq"),
            P("fsdp", None),
            P("fsdp", None),
            P("fsdp"),
        ),
        out_specs=(P("fsdp", "seq", None), P("fsdp", "seq"), P("fsdp", None), P("fsdp", None)),
        check_vma=False,
    )
```

time: 146 us -> 123 us (0.84)
  Pallas kernels: 134 us -> 117 us
  local copies, waits for them, and re-layouts: 9.93 us -> 4.31 us
    pallas_call x3 -> x1, Pallas kernels: 134 us -> 117 us  [run(): pl.pallas_call(whole_kernel, out_shape=(shape((ROWS, FEATURES), BF16), sh...]
    unnamed x22 -> x10, local copies, waits for them, and re-layouts: 9.93 us -> 4.31 us
where the time goes in v2:
time: 123 us
  Pallas kernels  117 us (95%)
  local copies, waits for them, and re-layouts  4.31 us (4%)
  between operations  1.31 us (1%)
    pallas_call x1, Pallas kernels, run(): pl.pallas_call(whole_kernel, out_shape=(shape((ROWS, FEATURES), BF16), sh...  117 us
    unnamed x10, local copies, waits for them, and re-layouts  4.31 us

profile of v2, /device:TPU:1, one launch (start us, length us, event | category | flops | bytes accessed | tf_op | source)
XLA Modules:
  0.0 122.6 jit_solution(13578718054591616883)
XLA Ops:
  1.3 117.0 %attention_backward.1 = (bf16[128,2048]{1,0:T(8,128)(2,1)}, f32[128,128]{1,0:T(8,128)}, f32[128,512]{1,0:T(8,128)}, f32[128,512]{1,0:T(8,128)}) custom-call(bf16[128,2048]{1,0:T(8,128)(2,1)} %bitcast.4, bf16[128,2048]{1,0:T(8,128)(2,1)} %bitcast.5, bf16[128,128]{1,0:T(8,128)(2,1)} %wq_hbm.1, bf16[128,512]{1,0:T(8,128)(2,1)} %wk_hbm.1, ...), custom_call_target="tpu_custom_call" | custom-call | tf_op jit(solution)/shard_map/attention_backward/pallas_call | solution.py:620
  118.3 0.0 copy-start.2
  118.3 0.0 copy-start.1
  118.3 1.9 %copy.17 = bf16[1,128,2048]{2,1,0:T(8,128)(2,1)} copy(bf16[1,128,2048]{2,1,0:T(8,128)(2,1)} %bitcast.3) | data formatting | bytes 1048576
  120.2 0.0 copy-done.2
  120.2 0.6 copy.18
  120.9 0.0 copy-done.1
  120.9 0.0 copy-start
  120.9 0.7 copy.19
  121.6 0.3 copy-done
  121.9 0.7 copy.20
Async XLA Ops:
  118.3 1.9 %copy-start.2 = (f32[128,128]{1,0:T(8,128)S(1)}, f32[128,128]{1,0:T(8,128)}, u32[]{:S(2)}) copy-start(f32[128,128]{1,0:T(8,128)} %get-tuple-element.17) | copy-start | bytes 196612
  118.3 2.6 %copy-start.1 = (f32[128,512]{1,0:T(8,128)S(1)}, f32[128,512]{1,0:T(8,128)}, u32[]{:S(2)}) copy-start(f32[128,512]{1,0:T(8,128)} %get-tuple-element.18) | copy-start | bytes 786436
  120.9 1.0 copy-start

commit v3 on v2

--- a/solution.py
+++ b/solution.py
@@ -26,13 +26,15 @@
     ("side", (0, 0), 64, 64, (0, 1)),
     ("up", (-1, 0), 0, 64, (2, 0)),
     ("down", (1, 0), 64, 64, (2, 0)),
-    ("side", (-1, 0), 0, 64, (-1, 1)),
-    ("side", (1, 0), 64, 64, (1, 1)),
+    ("side", (-1, 0), 0, 48, (-1, 1)),
+    ("side", (1, 0), 80, 48, (1, 1)),
     ("down", (0, 1), 0, 64, (1, 1)),
     ("up", (0, 1), 64, 64, (-1, 1)),
     ("up", (-1, 1), 0, 48, (2, 1)),
     ("down", (1, 1), 80, 48, (2, 1)),
     ("side", (2, 0), 48, 32, (2, 1)),
+    ("side", (-1, 0), 48, 16, (-1, 1)),
+    ("side", (1, 0), 64, 16, (1, 1)),
 )
 
 REDUCE = (
@@ -41,8 +43,10 @@
     ("side", (2, 1), 48, 32, (2, 0)),
     ("down", (-1, 1), 64, 64, (0, 1)),
     ("up", (1, 1), 0, 64, (0, 1)),
-    ("side", (-1, 1), 0, 64, (-1, 0)),
-    ("side", (1, 1), 64, 64, (1, 0)),
+    ("side", (-1, 1), 48, 16, (-1, 0)),
+    ("side", (1, 1), 64, 16, (1, 0)),
+    ("side", (-1, 1), 0, 48, (-1, 0)),
+    ("side", (1, 1), 80, 48, (1, 0)),
     ("down", (2, 0), 0, 64, (-1, 0)),
     ("up", (2, 0), 64, 64, (1, 0)),
     ("down", (-1, 0), 64, 64, (0, 0)),
@@ -52,7 +56,7 @@
     ("down", (-1, 0), 0, 64, (0, 0)),
     ("up", (1, 0), 64, 64, (0, 0)),
 )
-LAST = ((0, (10, 11, 13)), (64, (9, 12, 14)))
+LAST = ((0, (12, 13, 15)), (64, (11, 14, 16)))
 
 
 class Place:
@@ -88,13 +92,21 @@
 def enter(me):
     barrier = pltpu.get_barrier_semaphore()
 
-    def greet(j, carry):
-        for device in ((me.f, lax.rem(me.s + j, N_SEQ)), (lax.rem(me.f + j, N_FSDP), me.s)):
-            pl.semaphore_signal(barrier, inc=1, device_id=device, device_id_type=MESH)
-        return carry
-
-    lax.fori_loop(1, N_SEQ, greet, 0)
-    pl.semaphore_wait(barrier, 2 * (N_SEQ - 1))
+    def greet(device):
+        pl.semaphore_signal(barrier, inc=1, device_id=device, device_id_type=MESH)
+
+    def greet_seq(j, carry):
+        greet((me.f, lax.rem(me.s + j, N_SEQ)))
+        return carry
+
+    def greet_z(j, carry):
+        greet((me.lo * 8 + lax.rem(me.z + j, 8), me.s))
+        return carry
+
+    lax.fori_loop(1, N_SEQ, greet_seq, 0)
+    lax.fori_loop(1, 8, greet_z, 0)
+    greet(me.to("lo"))
+    pl.semaphore_wait(barrier, N_SEQ - 1 + 8)
 
 
 def remote(src, dst, send, recv, device):
@@ -113,8 +125,8 @@
     ((1, 0), (1, 4)),
     ((0, 1), (2, 5)),
     ((2, 0), (6, 7)),
-    ((-1, 1), (8, 11)),
-    ((1, 1), (9, 10)),
+    ((-1, 1), (8, 11, 15)),
+    ((1, 1), (9, 10, 16)),
     ((2, 1), (12, 13, 14)),
 )
 
@@ -159,28 +171,39 @@
         piece = w_piece(lo, z)
         return remote(piece, piece, w_send.at[slot], w_recv.at[slot], device)
 
-    def w_push(j, other):
+    def along(dz):
+        return (me.lo * 8 + lax.rem(me.z + dz + 8, 8), me.s)
+
+    def w_move(other, held, hop):
         lo = 1 - me.lo if other else me.lo
-        return w_copy(lo, me.z, 8 * other + j, (me.lo * 8 + lax.rem(me.z + j, 8), me.s))
+        return w_copy(lo, lax.rem(me.z + held + 8, 8), 9 * other + 4 + hop - held, along(hop))
+
+    def w_arrival(other, away):
+        lo = 1 - me.lo if other else me.lo
+        return w_copy(lo, lax.rem(me.z + away + 8, 8), 9 * other + 4 - away, along(1))
+
+    first_moves = [(0, hop) for hop in (1, -1, 2, -2)]
+    next_moves = {0: ((-2, 1), (2, -1), (-2, 2)), 1: ((-2, 1), (2, -1), (2, -2))}
 
     def w_start(other):
-        def step(j, carry):
-            w_push(j, other).start()
-            return carry
-
-        lax.fori_loop(1, 8, step, 0)
-
-    def w_finish(j, carry):
-        back = lax.rem(me.z + 8 - j, 8)
+        for held, hop in first_moves:
+            w_move(other, held, hop).start()
+
+    def w_onward(other):
+        w_arrival(other, -2).wait_recv()
+        w_arrival(other, 2).wait_recv()
+        for held, hop in next_moves[other]:
+            w_move(other, held, hop).start()
+
+    def w_finish():
         for other in (0, 1):
-            lo = 1 - me.lo if other else me.lo
-            w_copy(lo, back, 8 * other + j, me.to("lo")).wait_recv()
-        return carry
-
-    def w_sent(j, carry):
+            for away in (-1, 1, -3, 3, -4 if other == 0 else 4):
+                w_arrival(other, away).wait_recv()
+
+    def w_sent():
         for other in (0, 1):
-            w_push(j, other).wait_send()
-        return carry
+            for held, hop in first_moves + list(next_moves[other]):
+                w_move(other, held, hop).wait_send()
 
     def part(rel, first, count, other_core=0):
         at = pl.multiple_of(me.block(rel, other_core) * ROWS + first, 16)
@@ -243,11 +266,11 @@
         x_start(i)
     loads[0].wait()
     loads[1].wait()
-    own_to_lo = w_copy(me.lo, me.z, 0, me.to("lo"))
+    own_to_lo = w_copy(me.lo, me.z, 4, me.to("lo"))
     own_to_lo.start()
     w_start(0)
     core_copy(len(GATHER)).start()
-    w_copy(1 - me.lo, me.z, 0, me.to("lo")).wait_recv()
+    w_copy(1 - me.lo, me.z, 4, me.to("lo")).wait_recv()
     w_start(1)
     x_arrived(0)
     x_start(6)
@@ -255,8 +278,12 @@
     x_arrived(1)
     x_start(7)
     x_start(9)
+    x_start(15)
+    x_start(16)
     x_arrived(2)
     x_start(10)
+    w_onward(0)
+    w_onward(1)
     x_arrived(5)
     x_start(11)
     x_arrived(3)
@@ -271,12 +298,12 @@
     lax.fori_loop(1, N_SEQ, g_start, 0)
     for load in loads[3:]:
         load.wait()
-    lax.fori_loop(1, 8, w_finish, 0)
+    w_finish()
     share = remote(
         w_ref.at[:, pl.ds(HEAD, HEAD)],
         w_ref.at[:, pl.ds(2 * HEAD, HEAD)],
-        w_send.at[8],
-        w_recv.at[8],
+        w_send.at[17],
+        w_recv.at[17],
         me.to("core"),
     )
     share.start()
@@ -286,6 +313,8 @@
         project(rel, parts)
     x_arrived(10)
     x_arrived(11)
+    x_arrived(15)
+    x_arrived(16)
     for rel, parts in CHIP_PARTS[4:6]:
         project(rel, parts)
     for i in CHIP_PARTS[6][1]:
@@ -301,7 +330,7 @@
     lax.fori_loop(1, N_SEQ, g_finish, 0)
     share.wait_send()
     own_to_lo.wait_send()
-    lax.fori_loop(1, 8, w_sent, 0)
+    w_sent()
     for i in range(len(GATHER)):
         x_copy(i).wait_send()
     for i in range(len(GATHER) + 1):
@@ -397,7 +426,7 @@
 
 def scatter(
     me, g_ref, w_ref, rows, in_ref, dq_ref, dk_ref, dv_ref,
-    mine, away, near, arrived, dwq, dwm, dwo, kv_near, f_in, kv_all,
+    mine, away, near, arrived, dwq, dwm, dwo, kv_near, f_in, lo_out, lo_in, kv_all,
     r_send, r_recv, n_send, n_recv, kv_sem, f_send, f_recv, a_send, a_recv,
 ):
     def partial_sum(rel, other_core):
@@ -447,7 +476,9 @@
             ).astype(jnp.bfloat16)
             for n, target in enumerate(targets):
                 for k in range(4):
-                    target[c * 4 + k] = part[n * HEAD : (n + 1) * HEAD, k * ROWS : (k + 1) * ROWS]
+                    target[lax.div(c, 2), lax.rem(c, 2) * 4 + k] = part[
+                        n * HEAD : (n + 1) * HEAD, k * ROWS : (k + 1) * ROWS
+                    ]
             return carry
 
         lax.fori_loop(0, FEATURES // 512, step, 0)
@@ -455,22 +486,42 @@
     kv_copy = remote(dwo, kv_near, kv_sem.at[0], kv_sem.at[1], me.to("core"))
 
     def f_copy(source, kind, j):
-        to = lax.rem(me.f + j, N_FSDP)
-        return remote(source.at[to], f_in.at[kind, j], f_send.at[kind, j], f_recv.at[kind, j], (to, me.s))
+        to = lax.rem(me.z + j, 8)
+        return remote(
+            source.at[:, to], f_in.at[kind, j], f_send.at[kind, j], f_recv.at[kind, j], (me.lo * 8 + to, me.s)
+        )
 
     def f_start(source, kind):
         def step(j, carry):
             f_copy(source, kind, j).start()
             return carry
 
-        lax.fori_loop(1, N_FSDP, step, 0)
+        lax.fori_loop(1, 8, step, 0)
+
+    def lo_copy(kind):
+        return remote(lo_out.at[kind], lo_in.at[kind], f_send.at[kind, 0], f_recv.at[kind, 0], me.to("lo"))
 
     def f_sum(source, kind):
-        def step(j, total):
+        def step(j, totals):
             f_copy(source, kind, j).wait()
-            return total + f_in[kind, j].astype(jnp.float32)
-
-        return lax.fori_loop(1, N_FSDP, step, source[me.f].astype(jnp.float32))
+            return (
+                totals[0] + f_in[kind, j, me.lo].astype(jnp.float32),
+                totals[1] + f_in[kind, j, 1 - me.lo].astype(jnp.float32),
+            )
+
+        own, other = lax.fori_loop(
+            1,
+            8,
+            step,
+            (source[me.lo, me.z].astype(jnp.float32), source[1 - me.lo, me.z].astype(jnp.float32)),
+        )
+        lo_out[kind] = other.astype(jnp.bfloat16)
+        lo_copy(kind).start()
+        return own
+
+    def f_total(own, kind):
+        lo_copy(kind).wait()
+        return own + lo_in[kind].astype(jnp.float32)
 
     chip = lax.div(me.s, 2)
 
@@ -501,51 +552,57 @@
     r_start(0, 1, 2)
     block_out((1, 1))
     block_in((-1, 1))
-    r_start(3)
+    r_start(3, 5)
+    block_in((1, 1))
+    r_start(4, 6)
     weights(HEAD, 2 * HEAD, (dwm, dwo))
     kv_copy.start()
-    block_in((1, 1))
-    r_start(4)
     block_out((2, 0))
-    weights(0, HEAD, (dwq,))
-    f_start(dwq, 0)
+    r_add(0)
+    r_start(7)
+    r_add(1)
+    r_start(8)
     kv_copy.wait_recv()
 
-    def kv_add(c, carry):
-        dwm[c] = (dwm[c].astype(jnp.float32) + kv_near[c].astype(jnp.float32)).astype(jnp.bfloat16)
-        return carry
-
-    lax.fori_loop(0, N_FSDP, kv_add, 0)
+    def kv_add(z, carry):
+        for lo in (0, 1):
+            dwm[lo, z] = (dwm[lo, z].astype(jnp.float32) + kv_near[lo, z].astype(jnp.float32)).astype(
+                jnp.bfloat16
+            )
+        return carry
+
+    lax.fori_loop(0, 8, kv_add, 0)
     f_start(dwm, 1)
-    r_add(0)
-    r_start(5)
-    r_add(1)
-    r_start(6)
     block_in((2, 0))
     r_add(2)
-    r_start(7, 8)
+    r_start(9, 10)
     block_out((-1, 0))
     block_out((1, 0))
     block_in((-1, 0))
-    r_start(9)
+    r_start(11)
     block_in((1, 0))
-    r_start(10)
+    r_start(12)
+    weights(0, HEAD, (dwq,))
+    f_start(dwq, 0)
     block_out((0, 1))
     block_out((0, 0))
     block_in((0, 1))
     r_add(3)
     r_add(4)
-    r_start(11, 12)
+    r_start(13, 14)
     block_in((0, 0))
     r_add(5)
     r_add(7)
-    r_start(13)
     r_add(6)
     r_add(8)
-    r_start(14)
-    kv_all[me.core, chip] = f_sum(dwm, 1).astype(jnp.bfloat16)
+    r_add(9)
+    r_start(15)
+    r_add(10)
+    r_start(16)
+    kv_own = f_sum(dwm, 1)
+    kv_all[me.core, chip] = f_total(kv_own, 1).astype(jnp.bfloat16)
     lax.fori_loop(1, 8, a_start, 0)
-    dq_ref[...] = f_sum(dwq, 0).T
+    q_own = f_sum(dwq, 0)
     lax.fori_loop(1, 8, a_arrived, 0)
     kv_mine, kv_theirs = kv_all.at[me.core], kv_all.at[1 - me.core]
     kv_share = remote(kv_mine, kv_mine, kv_sem.at[2], kv_sem.at[3], me.to("core"))
@@ -556,6 +613,7 @@
             r_copy(i).wait_recv()
             total = total + arrived[pl.ds(RECV_AT[i], 64), :].astype(jnp.float32)
         in_ref[pl.ds(first, 64), :] = total.astype(jnp.bfloat16)
+    dq_ref[...] = f_total(q_own, 0).T
     remote(kv_theirs, kv_theirs, kv_sem.at[2], kv_sem.at[3], me.to("core")).wait_recv()
     for n in range(4):
         at = pl.ds(n * HEAD, HEAD)
@@ -577,7 +635,7 @@
     in_ref, dq_ref, dk_ref, dv_ref,
     rows, q_ref, k_ref, v_ref, grad_ref, w_ref, cos_ref, sin_ref,
     sc, dp_sc, dk_sc, dv_sc, kt_sc, cols,
-    mine, away, near, arrived, dwq, dwm, dwo, kv_near, f_in, kv_all,
+    mine, away, near, arrived, dwq, dwm, dwo, kv_near, f_in, lo_out, lo_in, kv_all,
     *sems,
 ):
     me = Place()
@@ -588,7 +646,7 @@
     attention(me, b_ref, q_ref, k_ref, v_ref, grad_ref, cos_ref, sin_ref, cols, sc, dp_sc, dk_sc, dv_sc, kt_sc)
     scatter(
         me, cols, w_ref, rows, in_ref, dq_ref, dk_ref, dv_ref,
-        mine, away, near, arrived, dwq, dwm, dwo, kv_near, f_in, kv_all, *sems[9:],
+        mine, away, near, arrived, dwq, dwm, dwo, kv_near, f_in, lo_out, lo_in, kv_all, *sems[9:],
     )
 
 
@@ -615,7 +673,8 @@
     table = pltpu.VMEM((LENGTH, HEAD), F32)
     scores = pltpu.VMEM((LENGTH, QB), F32)
     blocks = pltpu.VMEM((8, ROWS, FEATURES), BF16)
-    pieces = pltpu.VMEM((N_FSDP, HEAD, ROWS), BF16)
+    pieces = pltpu.VMEM((2, 8, HEAD, ROWS), BF16)
+    pair = pltpu.VMEM((2, HEAD, ROWS), BF16)
     hbm = pl.BlockSpec(memory_space=pltpu.HBM)
     return pl.pallas_call(
         whole_kernel,
@@ -650,7 +709,9 @@
             pieces,
             pieces,
             pieces,
-            pltpu.VMEM((2, N_FSDP, HEAD, ROWS), BF16),
+            pltpu.VMEM((2, 8, 2, HEAD, ROWS), BF16),
+            pair,
+            pair,
             pltpu.VMEM((2, 8, HEAD, ROWS), BF16),
             dma((len(GATHER),)),
             dma((len(GATHER),)),
@@ -658,16 +719,16 @@
             dma((len(GATHER) + 1,)),
             dma((N_SEQ,)),
             dma((N_SEQ,)),
-            dma((16,)),
-            dma((16,)),
+            dma((18,)),
+            dma((18,)),
             dma((6,)),
             dma((len(REDUCE),)),
             dma((len(REDUCE),)),
             dma((len(ORDER),)),
             dma((len(ORDER),)),
             dma((4,)),
-            dma((2, N_FSDP)),
-            dma((2, N_FSDP)),
+            dma((2, 8)),
+            dma((2, 8)),
             dma((8,)),
             dma((8,)),
         ],
@@ -676,12 +737,35 @@
     )(x, g, wq, wk, wv, cos, sin, boundary)
 
 
+def copy_kernel(*refs):
+    ins, outs, sem = refs[:4], refs[4:8], refs[8]
+    copies = [pltpu.make_async_copy(a, b, sem.at[n]) for n, (a, b) in enumerate(zip(ins, outs))]
+    for copy in copies:
+        copy.start()
+    for copy in copies:
+        copy.wait()
+
+
+def place_outputs(*arrays):
+    hbm = pl.BlockSpec(memory_space=pltpu.HBM)
+    return pl.pallas_call(
+        copy_kernel,
+        out_shape=tuple(shape(a.shape, a.dtype) for a in arrays),
+        in_specs=[hbm] * 4,
+        out_specs=(hbm,) * 4,
+        scratch_shapes=[dma((4,))],
+        compiler_params=pltpu.CompilerParams(vmem_limit_bytes=VMEM_LIMIT),
+        name="place_outputs",
+    )(*arrays)
+
+
 def shards(normed_input, out_grad, w_query, key_weight_matrix, value_weight_matrix, boundary):
     cos, sin = rope_tables()
     input_grad, dq, dk, dv = run(
         normed_input[0], out_grad[0], w_query, key_weight_matrix, value_weight_matrix,
         jnp.asarray(cos), jnp.asarray(sin), boundary,
     )
+    input_grad, dq, dk, dv = place_outputs(input_grad, dq, dk, dv)
     return (input_grad[None], dq, dk, dv)
 
 

time: 123 us -> 140 us (1.14)
  Pallas kernels: 117 us -> 138 us
  local copies, waits for them, and re-layouts: 4.31 us -> 0 us
    pallas_call x0 -> x1, Pallas kernels: none -> 34.9 us  [place_outputs(): pl.pallas_call(copy_kernel, out_shape=tuple((shape(a.shape, a.dtype) for...]
    pallas_call x1, Pallas kernels: 117 us -> 103 us  [run(): pl.pallas_call(whole_kernel, out_shape=(shape((ROWS, FEATURES), BF16), sh...]
    unnamed x10 -> x0, local copies, waits for them, and re-layouts: 4.31 us -> none
where the time goes in v3:
time: 140 us
  Pallas kernels  138 us (99%)
  between operations  1.47 us (1%)
    pallas_call x1, Pallas kernels, run(): pl.pallas_call(whole_kernel, out_shape=(shape((ROWS, FEATURES), BF16), sh...  103 us
    pallas_call x1, Pallas kernels, place_outputs(): pl.pallas_call(copy_kernel, out_shape=tuple((shape(a.shape, a.dtype) for...  34.9 us

profile of v3, /device:TPU:1, one launch (start us, length us, event | category | flops | bytes accessed | tf_op | source)
XLA Modules:
  0.0 139.7 jit_solution(8906267025291910032)
XLA Ops:
  1.3 103.3 %attention_backward.1 = (bf16[128,2048]{1,0:T(8,128)(2,1)}, f32[128,128]{1,0:T(8,128)}, f32[128,512]{1,0:T(8,128)}, f32[128,512]{1,0:T(8,128)}) custom-call(bf16[128,2048]{1,0:T(8,128)(2,1)} %bitcast.3, bf16[128,2048]{1,0:T(8,128)(2,1)} %bitcast.4, bf16[128,128]{1,0:T(8,128)(2,1)} %wq_hbm.1, bf16[128,512]{1,0:T(8,128)(2,1)} %wk_hbm.1, ...), custom_call_target="tpu_custom_call" | custom-call | tf_op jit(solution)/shard_map/attention_backward/pallas_call | solution.py:679
  104.6 34.9 %place_outputs.1 = (bf16[128,2048]{1,0:T(8,128)(2,1)}, f32[128,128]{1,0:T(8,128)}, f32[128,512]{1,0:T(8,128)}, f32[128,512]{1,0:T(8,128)}) custom-call(bf16[128,2048]{1,0:T(8,128)(2,1)} %get-tuple-element.12.refs_0_, f32[128,128]{1,0:T(8,128)} %get-tuple-element.13.refs_1_, f32[128,512]{1,0:T(8,128)} %get-tuple-element.14.refs_2_, ...), custom_call_target="tpu_custom_call" | custom-call | tf_op jit(solution)/shard_map/place_outputs/pallas_call | solution.py:751

commit v4 on v3

--- a/solution.py
+++ b/solution.py
@@ -738,22 +738,16 @@
 
 
 def copy_kernel(*refs):
-    ins, outs, sem = refs[:4], refs[4:8], refs[8]
-    copies = [pltpu.make_async_copy(a, b, sem.at[n]) for n, (a, b) in enumerate(zip(ins, outs))]
-    for copy in copies:
-        copy.start()
-    for copy in copies:
-        copy.wait()
+    for source, target in zip(refs[:4], refs[4:]):
+        target[...] = source[...]
 
 
 def place_outputs(*arrays):
-    hbm = pl.BlockSpec(memory_space=pltpu.HBM)
     return pl.pallas_call(
         copy_kernel,
         out_shape=tuple(shape(a.shape, a.dtype) for a in arrays),
-        in_specs=[hbm] * 4,
-        out_specs=(hbm,) * 4,
-        scratch_shapes=[dma((4,))],
+        in_specs=[vmem()] * 4,
+        out_specs=(vmem(),) * 4,
         compiler_params=pltpu.CompilerParams(vmem_limit_bytes=VMEM_LIMIT),
         name="place_outputs",
     )(*arrays)

time: 140 us -> 107 us (0.76)
  Pallas kernels: 138 us -> 106 us
    pallas_call x1, Pallas kernels: 34.9 us -> 2.23 us  [place_outputs(): pl.pallas_call(copy_kernel, out_shape=tuple((shape(a.shape, a.dtype) for...]
where the time goes in v4:
time: 107 us
  Pallas kernels  106 us (99%)
  between operations  1.29 us (1%)
    pallas_call x1, Pallas kernels, run(): pl.pallas_call(whole_kernel, out_shape=(shape((ROWS, FEATURES), BF16), sh...  103 us
    pallas_call x1, Pallas kernels, place_outputs(): pl.pallas_call(copy_kernel, out_shape=tuple((shape(a.shape, a.dtype) for...  2.23 us

profile of v4, /device:TPU:1, one launch (start us, length us, event | category | flops | bytes accessed | tf_op | source)
XLA Modules:
  0.0 106.8 jit_solution(13859272096406447180)
XLA Ops:
  1.3 103.3 %attention_backward.1 = (bf16[128,2048]{1,0:T(8,128)(2,1)}, f32[128,128]{1,0:T(8,128)}, f32[128,512]{1,0:T(8,128)}, f32[128,512]{1,0:T(8,128)}) custom-call(bf16[128,2048]{1,0:T(8,128)(2,1)} %bitcast.3, bf16[128,2048]{1,0:T(8,128)(2,1)} %bitcast.4, bf16[128,128]{1,0:T(8,128)(2,1)} %wq_hbm.1, bf16[128,512]{1,0:T(8,128)(2,1)} %wk_hbm.1, ...), custom_call_target="tpu_custom_call" | custom-call | tf_op jit(solution)/shard_map/attention_backward/pallas_call | solution.py:679
  104.6 2.2 %place_outputs.1 = (bf16[128,2048]{1,0:T(8,128)(2,1)}, f32[128,128]{1,0:T(8,128)}, f32[128,512]{1,0:T(8,128)}, f32[128,512]{1,0:T(8,128)}) custom-call(bf16[128,2048]{1,0:T(8,128)(2,1)} %get-tuple-element.12.refs_0_, f32[128,128]{1,0:T(8,128)} %get-tuple-element.13.refs_1_, f32[128,512]{1,0:T(8,128)} %get-tuple-element.14.refs_2_, ...), custom_call_target="tpu_custom_call" | custom-call | tf_op jit(solution)/shard_map/place_outputs/pallas_call | solution.py:746

commit v5 on v4

--- a/solution.py
+++ b/solution.py
@@ -262,12 +262,12 @@
         k_ref[at, :] = (k * cos + pltpu.roll(k, HEAD // 2, 1) * sin).astype(jnp.bfloat16)
         v_ref[at, :] = v.astype(jnp.bfloat16)
 
-    for i in range(6):
-        x_start(i)
     loads[0].wait()
     loads[1].wait()
     own_to_lo = w_copy(me.lo, me.z, 4, me.to("lo"))
     own_to_lo.start()
+    for i in range(6):
+        x_start(i)
     w_start(0)
     core_copy(len(GATHER)).start()
     w_copy(1 - me.lo, me.z, 4, me.to("lo")).wait_recv()
@@ -282,10 +282,10 @@
     x_start(16)
     x_arrived(2)
     x_start(10)
+    x_arrived(5)
+    x_start(11)
     w_onward(0)
     w_onward(1)
-    x_arrived(5)
-    x_start(11)
     x_arrived(3)
     x_arrived(4)
     x_arrived(8)
@@ -307,14 +307,14 @@
         me.to("core"),
     )
     share.start()
+    x_arrived(10)
+    x_arrived(11)
+    x_arrived(15)
+    x_arrived(16)
     share.wait_recv()
     project((0, 0), (len(GATHER),))
     for rel, parts in CHIP_PARTS[:4]:
         project(rel, parts)
-    x_arrived(10)
-    x_arrived(11)
-    x_arrived(15)
-    x_arrived(16)
     for rel, parts in CHIP_PARTS[4:6]:
         project(rel, parts)
     for i in CHIP_PARTS[6][1]:
@@ -339,7 +339,7 @@
 
 NT = (((1,), (1,)), ((), ()))
 TN = (((0,), (0,)), ((), ()))
-QB = 256
+QB = 512
 
 
 def attention(me, b_ref, q_ref, k_ref, v_ref, g_ref, cos_ref, sin_ref, out_ref, sc, dp_sc, dk_sc, dv_sc, kt_sc):
@@ -426,33 +426,33 @@
 
 def scatter(
     me, g_ref, w_ref, rows, in_ref, dq_ref, dk_ref, dv_ref,
-    mine, away, near, arrived, dwq, dwm, dwo, kv_near, f_in, lo_out, lo_in, kv_all,
+    both, near, arrived, dwq, dwm, dwo, kv_near, f_in, lo_out, lo_in, kv_all,
     r_send, r_recv, n_send, n_recv, kv_sem, f_send, f_recv, a_send, a_recv,
 ):
-    def partial_sum(rel, other_core):
-        at = pl.ds(pl.multiple_of(me.block(rel, other_core) * ROWS, ROWS), ROWS)
-        return lax.dot_general(
-            g_ref[at, :], w_ref[...], NT, preferred_element_type=jnp.float32
-        ).astype(jnp.bfloat16)
-
     def near_copy(n):
-        return remote(away.at[n], near.at[n], n_send.at[n], n_recv.at[n], me.to("core"))
+        return remote(both.at[n, 1 - me.core], near.at[n], n_send.at[n], n_recv.at[n], me.to("core"))
 
     def block_out(rel):
         n = SLOT[rel]
-        away[n] = partial_sum(rel, 1)
+        chip_rows = pl.ds(pl.multiple_of(lax.div(me.block(rel), 2) * 2 * ROWS, 2 * ROWS), 2 * ROWS)
+        part = lax.dot_general(
+            g_ref[chip_rows, :], w_ref[...], NT, preferred_element_type=jnp.float32
+        ).astype(jnp.bfloat16)
+        both[n, 0] = part[:ROWS]
+        both[n, 1] = part[ROWS:]
         near_copy(n).start()
-        mine[n] = partial_sum(rel, 0)
 
     def block_in(rel):
         n = SLOT[rel]
         near_copy(n).wait_recv()
-        mine[n] = (mine[n].astype(jnp.float32) + near[n].astype(jnp.float32)).astype(jnp.bfloat16)
+        both[n, me.core] = (both[n, me.core].astype(jnp.float32) + near[n].astype(jnp.float32)).astype(
+            jnp.bfloat16
+        )
 
     def r_copy(i):
         direction, rel, first, count, _ = REDUCE[i]
         return remote(
-            mine.at[SLOT[rel], pl.ds(first, count), :],
+            both.at[SLOT[rel], me.core, pl.ds(first, count), :],
             arrived.at[pl.ds(RECV_AT[i], count), :],
             r_send.at[i],
             r_recv.at[i],
@@ -463,8 +463,8 @@
         _, _, first, count, rel = REDUCE[i]
         r_copy(i).wait_recv()
         n = SLOT[rel]
-        mine[n, pl.ds(first, count), :] = (
-            mine[n, pl.ds(first, count), :].astype(jnp.float32)
+        both[n, me.core, pl.ds(first, count), :] = (
+            both[n, me.core, pl.ds(first, count), :].astype(jnp.float32)
             + arrived[pl.ds(RECV_AT[i], count), :].astype(jnp.float32)
         ).astype(jnp.bfloat16)
 
@@ -608,7 +608,7 @@
     kv_share = remote(kv_mine, kv_mine, kv_sem.at[2], kv_sem.at[3], me.to("core"))
     kv_share.start()
     for first, pieces in LAST:
-        total = mine[SLOT[(0, 0)], pl.ds(first, 64), :].astype(jnp.float32)
+        total = both[SLOT[(0, 0)], me.core, pl.ds(first, 64), :].astype(jnp.float32)
         for i in pieces:
             r_copy(i).wait_recv()
             total = total + arrived[pl.ds(RECV_AT[i], 64), :].astype(jnp.float32)
@@ -635,7 +635,7 @@
     in_ref, dq_ref, dk_ref, dv_ref,
     rows, q_ref, k_ref, v_ref, grad_ref, w_ref, cos_ref, sin_ref,
     sc, dp_sc, dk_sc, dv_sc, kt_sc, cols,
-    mine, away, near, arrived, dwq, dwm, dwo, kv_near, f_in, lo_out, lo_in, kv_all,
+    both, near, arrived, dwq, dwm, dwo, kv_near, f_in, lo_out, lo_in, kv_all,
     *sems,
 ):
     me = Place()
@@ -646,7 +646,7 @@
     attention(me, b_ref, q_ref, k_ref, v_ref, grad_ref, cos_ref, sin_ref, cols, sc, dp_sc, dk_sc, dv_sc, kt_sc)
     scatter(
         me, cols, w_ref, rows, in_ref, dq_ref, dk_ref, dv_ref,
-        mine, away, near, arrived, dwq, dwm, dwo, kv_near, f_in, lo_out, lo_in, kv_all, *sems[9:],
+        both, near, arrived, dwq, dwm, dwo, kv_near, f_in, lo_out, lo_in, kv_all, *sems[9:],
     )
 
 
@@ -701,8 +701,7 @@
             table,
             pltpu.VMEM((HEAD, LENGTH), BF16),
             pltpu.VMEM((LENGTH, 3 * HEAD), BF16),
-            blocks,
-            blocks,
+            pltpu.VMEM((8, 2, ROWS, FEATURES), BF16),
             blocks,
             pltpu.VMEM((RECV_ROWS, FEATURES), BF16),
             pieces,

time: 107 us -> 104 us (0.972)
  Pallas kernels: 106 us -> 103 us
    pallas_call x1, Pallas kernels: 103 us -> 101 us  [run(): pl.pallas_call(whole_kernel, out_shape=(shape((ROWS, FEATURES), BF16), sh...]
where the time goes in v5:
time: 104 us
  Pallas kernels  103 us (99%)
  between operations  1.29 us (1%)
    pallas_call x1, Pallas kernels, run(): pl.pallas_call(whole_kernel, out_shape=(shape((ROWS, FEATURES), BF16), sh...  101 us
    pallas_call x1, Pallas kernels, place_outputs(): pl.pallas_call(copy_kernel, out_shape=tuple((shape(a.shape, a.dtype) for...  2.23 us

profile of v5, /device:TPU:1, one launch (start us, length us, event | category | flops | bytes accessed | tf_op | source)
XLA Modules:
  0.0 104.4 jit_solution(7269463213833960629)
XLA Ops:
  1.3 100.9 %attention_backward.1 = (bf16[128,2048]{1,0:T(8,128)(2,1)}, f32[128,128]{1,0:T(8,128)}, f32[128,512]{1,0:T(8,128)}, f32[128,512]{1,0:T(8,128)}) custom-call(bf16[128,2048]{1,0:T(8,128)(2,1)} %bitcast.3, bf16[128,2048]{1,0:T(8,128)(2,1)} %bitcast.4, bf16[128,128]{1,0:T(8,128)(2,1)} %wq_hbm.1, bf16[128,512]{1,0:T(8,128)(2,1)} %wk_hbm.1, ...), custom_call_target="tpu_custom_call" | custom-call | tf_op jit(solution)/shard_map/attention_backward/pallas_call | solution.py:679
  102.1 2.2 %place_outputs.1 = (bf16[128,2048]{1,0:T(8,128)(2,1)}, f32[128,128]{1,0:T(8,128)}, f32[128,512]{1,0:T(8,128)}, f32[128,512]{1,0:T(8,128)}) custom-call(bf16[128,2048]{1,0:T(8,128)(2,1)} %get-tuple-element.12.refs_0_, f32[128,128]{1,0:T(8,128)} %get-tuple-element.13.refs_1_, f32[128,512]{1,0:T(8,128)} %get-tuple-element.14.refs_2_, ...), custom_call_target="tpu_custom_call" | custom-call | tf_op jit(solution)/shard_map/place_outputs/pallas_call | solution.py:745

commit v6 on v5

--- a/solution.py
+++ b/solution.py
@@ -106,7 +106,7 @@
     lax.fori_loop(1, N_SEQ, greet_seq, 0)
     lax.fori_loop(1, 8, greet_z, 0)
     greet(me.to("lo"))
-    pl.semaphore_wait(barrier, N_SEQ - 1 + 8)
+    return barrier
 
 
 def remote(src, dst, send, recv, device):
@@ -136,6 +136,7 @@
     rows, q_ref, k_ref, v_ref, grad_ref, w_ref,
     cos_ref, sin_ref, x_send, x_recv, c_send, c_recv, g_send, g_recv, w_send, w_recv, l_sem,
 ):
+    barrier = enter(me)
     own = pl.multiple_of(me.s * ROWS, ROWS)
     head_col = pl.multiple_of(me.y * HEAD, HEAD)
     own_w = pl.ds(pl.multiple_of(me.f * ROWS, ROWS), ROWS)
@@ -161,7 +162,7 @@
     for load in loads[3:]:
         load.start()
 
-    enter(me)
+    pl.semaphore_wait(barrier, N_SEQ - 1 + 8)
 
     def w_piece(lo, z):
         at = pl.multiple_of((lo * 8 + z) * ROWS, ROWS)
@@ -374,7 +375,6 @@
         for j in range(i + 1):
             at = pl.ds(j * QB, QB)
             p = sc[at, :] * inverse
-            sc[at, :] = p
             low_p = p.astype(jnp.bfloat16)
             d = lax.dot_general(v_ref[at, :], g, NT, preferred_element_type=jnp.float32)
             dp_sc[at, :] = d
@@ -387,7 +387,7 @@
         dq = jnp.zeros((HEAD, QB), jnp.float32)
         for j in range(i + 1):
             at = pl.ds(j * QB, QB)
-            ds = (sc[at, :] * (dp_sc[at, :] - delta)).astype(jnp.bfloat16)
+            ds = (sc[at, :] * inverse * (dp_sc[at, :] - delta)).astype(jnp.bfloat16)
             dk = jnp.dot(ds, q, preferred_element_type=jnp.float32)
             if j == i:
                 dk_sc[at, :] = dk
@@ -582,9 +582,9 @@
     r_start(11)
     block_in((1, 0))
     r_start(12)
+    block_out((0, 1))
     weights(0, HEAD, (dwq,))
     f_start(dwq, 0)
-    block_out((0, 1))
     block_out((0, 0))
     block_in((0, 1))
     r_add(3)

time: 104 us -> 103 us (level)
    pallas_call x1, Pallas kernels: 101 us -> 99.4 us  [run(): pl.pallas_call(whole_kernel, out_shape=(shape((ROWS, FEATURES), BF16), sh...]
where the time goes in v6:
time: 103 us
  Pallas kernels  102 us (99%)
  between operations  1.29 us (1%)
    pallas_call x1, Pallas kernels, run(): pl.pallas_call(whole_kernel, out_shape=(shape((ROWS, FEATURES), BF16), sh...  99.4 us
    pallas_call x1, Pallas kernels, place_outputs(): pl.pallas_call(copy_kernel, out_shape=tuple((shape(a.shape, a.dtype) for...  2.23 us

profile of v6, /device:TPU:1, one launch (start us, length us, event | category | flops | bytes accessed | tf_op | source)
XLA Modules:
  0.0 102.9 jit_solution(1113322561251826593)
XLA Ops:
  1.3 99.4 %attention_backward.1 = (bf16[128,2048]{1,0:T(8,128)(2,1)}, f32[128,128]{1,0:T(8,128)}, f32[128,512]{1,0:T(8,128)}, f32[128,512]{1,0:T(8,128)}) custom-call(bf16[128,2048]{1,0:T(8,128)(2,1)} %bitcast.3, bf16[128,2048]{1,0:T(8,128)(2,1)} %bitcast.4, bf16[128,128]{1,0:T(8,128)(2,1)} %wq_hbm.1, bf16[128,512]{1,0:T(8,128)(2,1)} %wk_hbm.1, ...), custom_call_target="tpu_custom_call" | custom-call | tf_op jit(solution)/shard_map/attention_backward/pallas_call | solution.py:679
  100.7 2.2 %place_outputs.1 = (bf16[128,2048]{1,0:T(8,128)(2,1)}, f32[128,128]{1,0:T(8,128)}, f32[128,512]{1,0:T(8,128)}, f32[128,512]{1,0:T(8,128)}) custom-call(bf16[128,2048]{1,0:T(8,128)(2,1)} %get-tuple-element.12.refs_0_, f32[128,128]{1,0:T(8,128)} %get-tuple-element.13.refs_1_, f32[128,512]{1,0:T(8,128)} %get-tuple-element.14.refs_2_, ...), custom_call_target="tpu_custom_call" | custom-call | tf_op jit(solution)/shard_map/place_outputs/pallas_call | solution.py:745
